TPU v7x, 512 devices: a whole 4x8x8 slice. The times are simulated.
512 devices in a mesh: seq: 16 (over y, core), label: 32 (over x, z).
Axes of the slice: x: 4, y: 8, z: 8, core: 2. Of those that a mesh axis runs over, the one named last changes fastest.
Arguments:
- hidden_states: bfloat16 [4096, 4096], P('seq', 'label'), may hold values from -6 to 6
- key_weight: bfloat16 [4096, 512], P('label'), may hold values from -0.09375 to 0.09375
- queries: bfloat16 [512, 32768], P('seq', 'label'), may hold values from -18 to 18
- output_weight: bfloat16 [512, 32768], P('seq', 'label'), may hold values from -0.59765625 to 0.59765625
- code_bias: float32 [32768], P('label'), may hold values from -6 to 6
- record_ids: int32 [4096], P('seq'), may hold values from 0 to 3, never falling along the last dimension, each value on 1 to 2048 neighbouring positions
- code_labels: int32 [4, 32768], P(None, 'label'), may hold values 0 or 1
Outputs:
- code_loss: float32 [4, 32768], P(None, 'label')
- grad_queries: float32 [512, 32768], P('seq', 'label')
- grad_output: float32 [512, 32768], P('seq', 'label')
- grad_bias: float32 [32768], P('label')
- grad_key_weight: float32 [4096, 512], P('label')
Inputs may be any that keep to these rules, and one draw needn't show every extreme that they name: `record_ids`: record ids never fall; every record has 1 to 2048 tokens, one exactly 2048.
All inputs are finite; a program needn't handle non-finite values. No bound on the sum of `code_labels` on one device may be relied on, other than what follows from the above.
Results may differ from a plain program's by a relative error of at most 0.015.
The roundings to bfloat16 on the way count: a program that leaves them out, or rounds other values in their place, can miss the bound.
Values may be sent and summed in bfloat16 or wider, within the bound.
No kernel may reach another device: no remote copies, remote signals or barrier semaphores. Data moves between devices by JAX's collectives and lax.ppermute only.
A program may use at most 64 MiB of HBM per device.

v0:
```python
import jax
import jax.numpy as jnp
from jax import lax
from jax.sharding import PartitionSpec as P


def on_device(
    hidden_states, key_weight, queries, output_weight, code_bias, record_ids, code_labels
):
    records = code_labels.shape[0]
    highest = lax.Precision.HIGHEST
    contract_rows = (((0,), (0,)), ((), ()))
    contract_cols = (((1,), (1,)), ((), ()))
    partial_pre = jnp.dot(hidden_states, key_weight, preferred_element_type=jnp.float32)
    tok_rows = partial_pre.shape[0]
    keys_all = jnp.tanh(lax.psum(partial_pre, "label")).astype(jnp.bfloat16)
    query_cols, output_cols = (
        lax.all_gather(queries, "seq", axis=0, tiled=True),
        lax.all_gather(output_weight, "seq", axis=0, tiled=True),
    )
    member = record_ids[:, None] == jnp.arange(records, dtype=jnp.int32)[None, :]
    onehot = member.astype(jnp.float32)
    code_width = query_cols.shape[1]
    span_codes = min(256, code_width)
    block_count = code_width // span_codes

    def scores(block_idx):
        lower = block_idx * span_codes
        query_blk = query_cols[:, lower : lower + span_codes]
        output_blk = output_cols[:, lower : lower + span_codes]
        score_vals = jnp.dot(keys_all, query_blk, preferred_element_type=jnp.float32)
        value_vals = jnp.dot(keys_all, output_blk, preferred_element_type=jnp.float32)
        return (score_vals, value_vals, query_blk, output_blk)

    computed = [scores(block_idx) for block_idx in range(block_count)]

    def record_max(score_vals):
        return jnp.stack(
            [
                jnp.max(jnp.where(member[:, rec : rec + 1], score_vals, -1e30), axis=0)
                for rec in range(records)
            ]
        )

    def spread(table):
        return jnp.dot(onehot, table, precision=highest)

    local_top = jnp.concatenate(
        [record_max(computed[block_idx][0]) for block_idx in range(block_count)], axis=1
    )
    record_top = lax.pmax(local_top, "seq")
    parts_den = []
    parts_num = []
    for block_idx in range(block_count):
        score_vals, value_vals, query_blk, output_blk = computed[block_idx]
        lower = block_idx * span_codes
        expo = jnp.exp(score_vals - spread(record_top[:, lower : lower + span_codes]))
        denoms = jnp.dot(onehot.T, expo, precision=highest)
        numers = jnp.dot(onehot.T, expo * value_vals, precision=highest)
        denoms, numers = (denoms, numers)
        parts_den.append(denoms)
        parts_num.append(numers)
    denoms, numers = lax.psum(
        (jnp.concatenate(parts_den, axis=1), jnp.concatenate(parts_num, axis=1)), "seq"
    )
    pooled = numers / denoms
    logits = pooled + code_bias[None, :]
    labels_f = code_labels.astype(jnp.float32)
    code_loss = jax.nn.softplus(logits) - labels_f * logits
    delta = jax.nn.sigmoid(logits) - labels_f
    grad_bias = jnp.sum(delta, axis=0)
    key_grad = jnp.zeros((tok_rows, query_cols.shape[0]), jnp.float32)
    query_parts = []
    output_parts = []
    for block_idx in range(block_count):
        score_vals, value_vals, query_blk, output_blk = computed[block_idx]
        lower = block_idx * span_codes
        upper = lower + span_codes
        attend = jnp.exp(score_vals - spread(record_top[:, lower:upper])) / spread(
            denoms[:, lower:upper]
        )
        pool_weight = spread(delta[:, lower:upper]) * attend
        pool_grad = pool_weight.astype(jnp.bfloat16)
        score_grad = (pool_weight * (value_vals - spread(pooled[:, lower:upper]))).astype(
            jnp.bfloat16
        )
        output_parts.append(
            lax.dot_general(keys_all, pool_grad, contract_rows, preferred_element_type=jnp.float32)
        )
        query_parts.append(
            lax.dot_general(keys_all, score_grad, contract_rows, preferred_element_type=jnp.float32)
        )
        key_grad = key_grad + lax.dot_general(
            score_grad, query_blk, contract_cols, preferred_element_type=jnp.float32
        )
        key_grad = key_grad + lax.dot_general(
            pool_grad, output_blk, contract_cols, preferred_element_type=jnp.float32
        )
    grad_queries, grad_output = (
        lax.psum_scatter(
            jnp.concatenate(query_parts, axis=1), "seq", scatter_dimension=0, tiled=True
        ),
        lax.psum_scatter(
            jnp.concatenate(output_parts, axis=1), "seq", scatter_dimension=0, tiled=True
        ),
    )
    keys_f = keys_all.astype(jnp.float32)
    summed_grad = lax.psum(key_grad, "label")
    pre_grad = (summed_grad * (1.0 - keys_f * keys_f)).astype(jnp.bfloat16)
    weight_part = lax.dot_general(
        hidden_states, pre_grad, contract_rows, preferred_element_type=jnp.float32
    )
    grad_key_weight = lax.psum(weight_part, "seq")
    return (code_loss, grad_queries, grad_output, grad_bias, grad_key_weight)


def solution(mesh):
    return jax.shard_map(
        on_device,
        mesh=mesh,
        in_specs=(
            P("seq", "label"),
            P("label", None),
            P("seq", "label"),
            P("seq", "label"),
            P("label"),
            P("seq"),
            P(None, "label"),
        ),
        out_specs=(
            P(None, "label"),
            P("seq", "label"),
            P("seq", "label"),
            P("label"),
            P("label", None),
        ),
        check_vma=False,
    )
```

profile of v0, /device:TPU:1, one launch (start us, length us, event | category | flops | bytes accessed | tf_op | source)
XLA Modules:
  0.0 697.9 jit_solution(13058000982854026971)
XLA Ops:
  8.1 0.8 copy-done
  8.9 1.9 fusion.113
  10.8 0.5 all-gather.3.cloned.1.call-update
  11.4 0.5 all-gather.5.cloned.1.call-update
  12.0 0.7 iota_compare_fusion
  12.7 159.7 %all-reduce.5.cloned.1.call-done = f32[256,512]{1,0:T(8,128)} async-done(((f32[256,512]{1,0:T(8,128)}), f32[256,512]{1,0:T(8,128)}) %all-reduce.5.cloned.1.call-update) | async-done | bytes 524304 | tf_op jit(solution)/shard_map/psum | solution.py:16
  172.4 1.1 tanh_convert_fusion
  173.6 1.3 fusion.41
  174.8 1.2 fusion.44
  176.0 1.2 fusion.48
  177.2 0.5 select_reduce_fusion.3
  177.8 47.3 %pmax.7 = f32[4,1024]{1,0:T(4,128)S(1)} all-reduce(f32[4,1024]{1,0:T(4,128)S(1)} %maximum_maximum_fusion), channel_id=1, replica_groups=mesh['seq'=16,'label'=32] {'seq'}, use_global_device_ids=true, to_apply=%region_17.18 | all-reduce | flops 4096 | bytes 32768 | tf_op jit(solution)/shard_map/pmax | solution.py:51
  225.1 0.3 fusion.8
  225.6 0.3 fusion.10
  226.0 0.3 fusion.9
  226.3 1.0 fusion.11
  227.4 1.3 fusion.35
  229.1 1.2 fusion.32
  231.9 0.6 pad_maximum_fusion.2
  232.5 46.3 %all-reduce = (f32[4,1024]{1,0:T(4,128)}, f32[4,1024]{1,0:T(4,128)}) all-reduce(f32[4,1024]{1,0:T(4,128)} %get-tuple-element.58, f32[4,1024]{1,0:T(4,128)} %get-tuple-element.59), channel_id=1, replica_groups=mesh['seq'=16,'label'=32] {'seq'}, use_global_device_ids=true, to_apply=%region_18.19 | all-reduce | flops 8192 | bytes 65536 | tf_op jit(solution)/shard_map/psum | solution.py:63
  278.8 1.4 fusion.112
  281.2 0.3 fusion.77
  281.6 1.3 fusion.1
  282.9 1.1 fusion.51
  284.0 0.3 fusion.15
  284.4 0.3 fusion.3
  284.7 0.3 fusion.14
  285.1 0.3 fusion.5
  285.4 0.3 fusion.13
  285.8 0.3 fusion.7
  286.1 0.3 fusion.12
  286.5 0.6 copy-done.11
  289.1 1.1 convolution_add_fusion
  290.2 1.1 fusion.54
  291.3 1.1 fusion.57
  292.4 1.1 fusion.60
  293.5 151.6 %all-reduce.7.cloned.1.call-done = f32[256,512]{1,0:T(8,128)} async-done(((f32[256,512]{1,0:T(8,128)}), f32[256,512]{1,0:T(8,128)}) %all-reduce.7.cloned.1.call-update) | async-done | bytes 524304 | tf_op jit(solution)/shard_map/psum | solution.py:108
  445.1 2.0 convolution_bitcast_fusion
  447.2 1.5 pad_maximum_fusion.1
  448.7 1.9 copy.23
  450.7 0.8 copy-done.14
  452.8 1.8 copy.21
  454.6 0.7 copy-done.22
  455.4 0.6 fusion.62
  456.0 105.8 %all-reduce.9.cloned.1.call-done = f32[128,512]{0,1:T(8,128)} async-done(((f32[128,512]{0,1:T(8,128)}), f32[128,512]{0,1:T(8,128)}) %all-reduce.9.cloned.1.call-update) | async-done | bytes 262160 | tf_op jit(solution)/shard_map/psum | solution.py:113
  561.7 1.8 copy.20
  563.5 62.7 %reduce-scatter.9.cloned.1.call-done = f32[32,1024]{1,0:T(8,128)} async-done(((f32[512,1024]{1,0:T(8,128)}), f32[32,1024]{1,0:T(8,128)}) %reduce-scatter.9.cloned.1.call-update) | async-done | bytes 131088
  626.2 64.1 %reduce-scatter.7.cloned.1.call-done = f32[32,1024]{1,0:T(8,128)} async-done(((f32[512,1024]{1,0:T(8,128)}), f32[32,1024]{1,0:T(8,128)}) %reduce-scatter.7.cloned.1.call-update) | async-done | bytes 131088
  (89 shorter events, 6.8 us)
Async XLA Ops:
  8.0 0.9 copy-start
  8.0 164.4 %all-reduce.5.cloned.1.call-start = ((), (), s32[]{:S(2)}) async-start(), calls=%async_computation.2 | async-start | bytes 1048576 | tf_op jit(solution)/shard_map/psum | solution.py:16
  10.8 162.8 %all-gather.3.cloned.1.call-start = ((), (), s32[]{:S(2)}) async-start(), calls=%async_computation.3 | async-start | bytes 1114112 | tf_op jit(solution)/shard_map/all_gather | solution.py:18
  11.4 216.0 %all-gather.5.cloned.1.call-start = ((), (), s32[]{:S(2)}) async-start(), calls=%async_computation.4 | async-start | bytes 1114112 | tf_op jit(solution)/shard_map/all_gather | solution.py:19
  12.0 433.1 %all-reduce.7.cloned.1.call-start = ((), (), s32[]{:S(2)}) async-start(), calls=%async_computation.5 | async-start | bytes 1048576 | tf_op jit(solution)/shard_map/psum | solution.py:108
  173.6 3.7 copy-start.2
  176.0 49.0 %copy-start.19 = (s32[256]{0:T(256)S(1)}, s32[256]{0:T(256)}, u32[]{:S(2)}) copy-start(s32[256]{0:T(256)} %param.12) | copy-start | bytes 3076
  225.4 3.5 copy-start.3
  226.0 5.0 copy-start.7
  226.3 4.2 copy-start.5
  227.4 3.4 copy-start.1
  227.4 3.8 copy-start.9
  230.3 48.5 %copy-start.25 = (f32[1024]{0:T(1024)S(1)}, f32[1024]{0:T(1024)}, u32[]{:S(2)}) copy-start(f32[1024]{0:T(1024)} %param.11) | copy-start | bytes 12292
  278.8 5.5 copy-start.8
  278.8 5.6 copy-start.24
  280.2 5.9 copy-start.21
  281.6 3.5 copy-start.6
  284.0 1.8 copy-start.4
  284.4 4.4 copy-start.13
  285.1 3.2 copy-start.15
  285.8 2.2 copy-start.17
  286.5 0.7 copy-start.11
  290.2 154.9 %copy-start.20 = (bf16[256,128]{1,0:T(8,128)(2,1)S(1)}, bf16[256,128]{1,0:T(8,128)(2,1)}, u32[]{:S(2)}) copy-start(bf16[256,128]{1,0:T(8,128)(2,1)} %param.7) | copy-start | bytes 196612
  290.2 271.5 %all-reduce.9.cloned.1.call-start = ((), (), s32[]{:S(2)}) async-start(), calls=%async_computation.6 | async-start | bytes 524288 | tf_op jit(solution)/shard_map/psum | solution.py:113
  292.4 154.8 %copy-start.10 = (f32[512,256]{0,1:T(8,128)S(1)}, f32[512,256]{0,1:T(8,128)}, u32[]{:S(2)}) copy-start(f32[512,256]{0,1:T(8,128)} %fusion.54) | copy-start | bytes 1572868
  447.1 179.1 %reduce-scatter.9.cloned.1.call-start = ((), (), s32[]{:S(2)}) async-start(), calls=%async_computation.8 | async-start | bytes 2228224
  450.6 0.9 copy-start.14
  450.6 1.2 copy-start.16
  450.6 1.5 copy-start.18
  450.6 1.7 copy-start.12
  450.6 239.7 %reduce-scatter.7.cloned.1.call-start = ((), (), s32[]{:S(2)}) async-start(), calls=%async_computation.7 | async-start | bytes 2228224
  454.6 0.7 copy-start.22
  454.6 0.7 copy-start.23
Sparse Core Ops, SparseCore 0:
  12.2 160.1 all-reduce.4
  290.3 154.6 all-reduce.6
Sparse Core Ops, SparseCore 1:
  13.6 46.9 all-gather.2
  62.8 40.0 all-gather.4
  447.2 114.5 all-reduce.8
  565.4 60.7 reduce-scatter.8
  629.8 60.4 reduce-scatter.6
where the time goes:
time: 699 us; the launch traced here: 698 us
  waiting for transfers between devices  545 us (78%)
  blocking collectives  93.6 us (13%)
  matrix products  28 us (4%)
  between operations  16.2 us (2%)
  local copies, waits for them, and re-layouts  8.64 us (1%)
    psum x1, waiting for transfers between devices, on_device(): keys_all = jnp.tanh(lax.psum(partial_pre, 'label')).astype(jnp.bfloat16)  160 us
    psum x1, waiting for transfers between devices, on_device(): summed_grad = lax.psum(key_grad, 'label')  152 us
    unnamed x9, waiting for transfers between devices  128 us
    psum x1, waiting for transfers between devices, on_device(): grad_key_weight = lax.psum(weight_part, 'seq')  106 us
    pmax x1, blocking collectives, on_device(): record_top = lax.pmax(local_top, 'seq')  47.3 us
    psum x1, blocking collectives, on_device(): lax.psum((jnp.concatenate(parts_den, axis=1), jnp.concatenate(parts_num,...  46.3 us
  transfers between devices with their start and end apart: 7, of which 5 were waited for; matrix products, arithmetic and copies ran while one was open for 3% of the time, Pallas kernels for 0%

commit v1 on v0

v1 whole, which is shorter than its diff:
```python
import jax
import jax.numpy as jnp
from jax import lax
from jax.experimental import pallas as pl
from jax.experimental.pallas import tpu as pltpu
from jax.sharding import PartitionSpec as P

FAR = -1e30
ROWS = (((0,), (0,)), ((), ()))
COLS = (((1,), (1,)), ((), ()))
SPAN = 256


def keys_kernel(parts_ref, out_ref):
    own = jnp.tanh(jnp.sum(parts_ref[...], axis=0)).astype(out_ref.dtype)
    out_ref[...] = jnp.broadcast_to(own[None], out_ref.shape)


def products(keys, query_ref, output_ref):
    query_blk = query_ref[...].reshape(-1, query_ref.shape[-1])
    output_blk = output_ref[...].reshape(-1, output_ref.shape[-1])
    score_vals = jnp.dot(keys, query_blk, preferred_element_type=jnp.float32)
    value_vals = jnp.dot(keys, output_blk, preferred_element_type=jnp.float32)
    return score_vals, value_vals, query_blk, output_blk


def spread(masks, rows):
    spread_vals = rows[-1]
    for mask, row in zip(masks[:-1], rows[:-1]):
        spread_vals = jnp.where(mask, row, spread_vals)
    return spread_vals


def totals_kernel(records, keys_ref, query_ref, output_ref, ids_ref, out_ref):
    score_vals, value_vals, _, _ = products(keys_ref[...], query_ref, output_ref)
    ids = ids_ref[...]
    masks = [ids == rec for rec in range(records)]
    tops = [
        jnp.max(jnp.where(mask, score_vals, FAR), axis=0, keepdims=True) for mask in masks
    ]
    expo = jnp.exp(score_vals - spread(masks, tops))
    weighted = expo * value_vals
    logs, means = [], []
    for mask, top in zip(masks, tops):
        denom = jnp.sum(jnp.where(mask, expo, 0.0), axis=0, keepdims=True)
        numer = jnp.sum(jnp.where(mask, weighted, 0.0), axis=0, keepdims=True)
        some = denom > 0.0
        safe = jnp.where(some, denom, 1.0)
        logs.append(jnp.where(some, top + jnp.log(safe), FAR))
        means.append(jnp.where(some, numer / safe, 0.0))
    table = jnp.concatenate(logs + means, axis=0)
    out_ref[...] = jnp.broadcast_to(table[None], out_ref.shape)


def grads_kernel(
    records,
    keys_ref,
    query_ref,
    output_ref,
    ids_ref,
    totals_ref,
    bias_ref,
    labels_ref,
    loss_ref,
    bias_grad_ref,
    grads_ref,
    key_grad_ref,
    sum_ref,
):
    step = pl.program_id(0)
    keys = keys_ref[...]
    score_vals, value_vals, query_blk, output_blk = products(keys, query_ref, output_ref)
    logs, pools = [], []
    for rec in range(records):
        log_parts = totals_ref[:, rec, :]
        mean_parts = totals_ref[:, records + rec, :]
        top = jnp.max(log_parts, axis=0, keepdims=True)
        weights = jnp.exp(log_parts - top)
        denom = jnp.sum(weights, axis=0, keepdims=True)
        logs.append(top + jnp.log(denom))
        pools.append(jnp.sum(weights * mean_parts, axis=0, keepdims=True) / denom)
    logits = jnp.concatenate(pools, axis=0) + bias_ref[...]
    labels_f = labels_ref[...].astype(jnp.float32)
    small = jnp.exp(-jnp.abs(logits))
    loss_ref[...] = jnp.maximum(logits, 0.0) + jnp.log1p(small) - labels_f * logits
    delta = jnp.where(logits >= 0.0, 1.0, small) / (1.0 + small) - labels_f
    bias_grad_ref[...] = jnp.sum(delta, axis=0, keepdims=True)
    ids = ids_ref[...]
    masks = [ids == rec for rec in range(records)]
    deltas = [delta[rec : rec + 1] for rec in range(records)]
    pool_weight = spread(masks, deltas) * jnp.exp(score_vals - spread(masks, logs))
    pool_grad = pool_weight.astype(jnp.bfloat16)
    score_grad = (pool_weight * (value_vals - spread(masks, pools))).astype(jnp.bfloat16)
    shape = (grads_ref.shape[0], grads_ref.shape[2], grads_ref.shape[3])
    grads_ref[:, 0] = lax.dot_general(
        keys, score_grad, ROWS, preferred_element_type=jnp.float32
    ).reshape(shape)
    grads_ref[:, 1] = lax.dot_general(
        keys, pool_grad, ROWS, preferred_element_type=jnp.float32
    ).reshape(shape)
    part = lax.dot_general(score_grad, query_blk, COLS, preferred_element_type=jnp.float32)
    part += lax.dot_general(pool_grad, output_blk, COLS, preferred_element_type=jnp.float32)

    @pl.when(step == 0)
    def _():
        sum_ref[...] = part

    @pl.when(step > 0)
    def _():
        sum_ref[...] += part

    @pl.when(step == pl.num_programs(0) - 1)
    def _():
        key_grad_ref[...] = sum_ref[...].astype(key_grad_ref.dtype)


def pre_grad_kernel(parts_ref, keys_ref, out_ref):
    keys_f = keys_ref[...].astype(jnp.float32)
    total = jnp.sum(parts_ref[...].astype(jnp.float32), axis=0)
    own = (total * (1.0 - keys_f * keys_f)).astype(out_ref.dtype)
    out_ref[...] = jnp.broadcast_to(own[None], out_ref.shape)


def sum_kernel(parts_ref, out_ref):
    own = jnp.sum(parts_ref[...].astype(jnp.float32), axis=0).astype(out_ref.dtype)
    out_ref[...] = jnp.broadcast_to(own[None], out_ref.shape)


def swap(parts, axis):
    return lax.all_to_all(parts, axis, 0, 0, tiled=True)


def struct(shape, dtype):
    return jax.ShapeDtypeStruct(shape, dtype)


def on_device(
    hidden_states, key_weight, queries, output_weight, code_bias, record_ids, code_labels
):
    f32, bf16 = jnp.float32, jnp.bfloat16
    records, width = code_labels.shape
    seq, label = lax.axis_size("seq"), lax.axis_size("label")
    tokens, feats = hidden_states.shape
    dims = key_weight.shape[1]
    rows = queries.shape[0]
    own_toks, own_feats = tokens // label, feats // seq

    vectors = lax.all_gather(jnp.stack([queries, output_weight]), "seq", axis=0)
    partial_pre = jnp.dot(hidden_states, key_weight, preferred_element_type=f32)
    pre_parts = swap(partial_pre.reshape(label, own_toks, dims), "label")
    keys_copies = pl.pallas_call(
        keys_kernel, out_shape=struct((label, own_toks, dims), bf16)
    )(pre_parts)
    keys_own = keys_copies[0]
    keys_all = swap(keys_copies, "label").reshape(tokens, dims)

    ids = record_ids[:, None]
    span = min(SPAN, width)
    grid = (width // span,)
    whole = lambda *shape: pl.BlockSpec(shape, lambda i: (0,) * len(shape))
    codes = lambda lead: pl.BlockSpec((lead, span), lambda i: (0, i))
    vector_specs = [
        pl.BlockSpec((seq, None, rows, span), lambda i: (0, 0, 0, i)),
        pl.BlockSpec((seq, None, rows, span), lambda i: (0, 1, 0, i)),
    ]
    totals_spec = pl.BlockSpec((seq, 2 * records, span), lambda i: (0, 0, i))
    params = pltpu.CompilerParams(vmem_limit_bytes=48 * 1024 * 1024)
    totals = pl.pallas_call(
        lambda *refs: totals_kernel(records, *refs),
        grid=grid,
        in_specs=[whole(tokens, dims), *vector_specs, whole(tokens, 1)],
        out_specs=totals_spec,
        out_shape=struct((seq, 2 * records, width), f32),
        compiler_params=params,
    )(keys_all, vectors, vectors, ids)
    totals = swap(totals, "seq")

    code_loss, grad_bias, grads, key_grad = pl.pallas_call(
        lambda *refs: grads_kernel(records, *refs),
        grid=grid,
        in_specs=[
            whole(tokens, dims),
            *vector_specs,
            whole(tokens, 1),
            totals_spec,
            codes(1),
            codes(records),
        ],
        out_specs=[
            codes(records),
            codes(1),
            pl.BlockSpec((seq, 2, rows, span), lambda i: (0, 0, 0, i)),
            whole(tokens, dims),
        ],
        out_shape=[
            struct((records, width), f32),
            struct((1, width), f32),
            struct((seq, 2, rows, width), f32),
            struct((tokens, dims), bf16),
        ],
        scratch_shapes=[pltpu.VMEM((tokens, dims), f32)],
        compiler_params=params,
    )(keys_all, vectors, vectors, ids, totals, code_bias[None], code_labels)

    grads = lax.psum_scatter(grads, "seq", scatter_dimension=0)
    grad_queries, grad_output = grads[0], grads[1]

    key_parts = swap(key_grad.reshape(label, own_toks, dims), "label")
    pre_copies = pl.pallas_call(
        pre_grad_kernel, out_shape=struct((label, own_toks, dims), bf16)
    )(key_parts, keys_own)
    pre_grad = swap(pre_copies, "label").reshape(tokens, dims)
    weight_part = lax.dot_general(
        hidden_states, pre_grad, ROWS, preferred_element_type=f32
    ).astype(bf16)
    weight_parts = swap(weight_part.reshape(seq, own_feats, dims), "seq")
    weight_copies = pl.pallas_call(
        sum_kernel, out_shape=struct((seq, own_feats, dims), bf16)
    )(weight_parts)
    grad_key_weight = swap(weight_copies, "seq").reshape(feats, dims).astype(f32)
    return (code_loss, grad_queries, grad_output, grad_bias[0], grad_key_weight)


def solution(mesh):
    return jax.shard_map(
        on_device,
        mesh=mesh,
        in_specs=(
            P("seq", "label"),
            P("label", None),
            P("seq", "label"),
            P("seq", "label"),
            P("label"),
            P("seq"),
            P(None, "label"),
        ),
        out_specs=(
            P(None, "label"),
            P("seq", "label"),
            P("seq", "label"),
            P("label"),
            P("label", None),
        ),
        check_vma=False,
    )
```

time: 699 us -> 170 us (0.24)
  waiting for transfers between devices: 545 us -> 20.7 us
  matrix products: 28 us -> 1.27 us
  Pallas kernels: 0 us -> 13.1 us
  starting transfers between devices: 0.3 us -> 13.1 us
    psum x3 -> x0, waiting for transfers between devices: 417 us -> none  [the longest x1 160 us: on_device(): keys_all = jnp.tanh(lax.psum(partial_pre, 'label')).astype(jnp.bfloat16)]
    unnamed x9 -> x2, waiting for transfers between devices: 128 us -> 0.03 us
    all_to_all x0 -> x5, blocking collectives: none -> 98.2 us  [swap(): return lax.all_to_all(parts, axis, 0, 0, tiled=True)]
    pmax x1 -> x0, blocking collectives: 47.3 us -> none  [on_device(): record_top = lax.pmax(local_top, 'seq')]
    psum x1 -> x0, blocking collectives: 46.3 us -> none  [on_device(): lax.psum((jnp.concatenate(parts_den, axis=1), jnp.concatenate(parts_num,...]
    dot_general x50 -> x2, matrix products: 28 us -> 1.27 us  [the longest x1 1.04 us: on_device(): partial_pre = jnp.dot(hidden_states, key_weight, preferred_element_type=f32)]
    all_to_all x0 -> x2, waiting for transfers between devices: none -> 18.8 us  [swap(): return lax.all_to_all(parts, axis, 0, 0, tiled=True)]
    pallas_call x0 -> x5, Pallas kernels: none -> 13.1 us  [the longest x1 4.98 us: on_device(): pl.pallas_call(lambda *refs: grads_kernel(records, *refs), grid=grid, in_...]
  transfers between devices with their start and end apart: 7 -> 4, of which waited for: 5 -> 3; matrix products, arithmetic and copies ran while one was open for 3% -> 2% of each run, Pallas kernels for 0% -> 3%
where the time goes in v1:
time: 170 us; the launch traced here: 169 us
  blocking collectives  98.2 us (58%)
  waiting for transfers between devices  20.7 us (12%)
  between operations  14.1 us (8%)
  starting transfers between devices  13.1 us (8%)
  Pallas kernels  13.1 us (8%)
  local copies, waits for them, and re-layouts  6.11 us (4%)
  other arithmetic  2.3 us (1%)
    all_to_all x5, blocking collectives, swap(): return lax.all_to_all(parts, axis, 0, 0, tiled=True)  98.2 us
    all_to_all x2, waiting for transfers between devices, swap(): return lax.all_to_all(parts, axis, 0, 0, tiled=True)  18.8 us
    all_to_all x2, starting transfers between devices, swap(): return lax.all_to_all(parts, axis, 0, 0, tiled=True)  13.1 us
    pallas_call x1, Pallas kernels, on_device(): pl.pallas_call(lambda *refs: grads_kernel(records, *refs), grid=grid, in_...  4.98 us
  transfers between devices with their start and end apart: 4, of which 3 were waited for; matrix products, arithmetic and copies ran while one was open for 2% of the time, Pallas kernels for 3%

profile of v1, /device:TPU:1, one launch (start us, length us, event | category | flops | bytes accessed | tf_op | source)
XLA Modules:
  0.0 169.0 jit_solution(8093383903697934538)
XLA Ops:
  7.2 0.0 copy-start
  7.2 0.0 all-gather.3.cloned.1.call-start
  7.2 1.6 pad_maximum_fusion
  8.8 0.0 all-gather.3.cloned.1.call-update
  8.8 0.0 copy-done
  8.8 1.0 convolution_bitcast_fusion
  9.9 0.0 copy-start.2
  9.9 0.0 copy-start.3
  9.9 27.9 %all_to_all.35.parts_ref = f32[32,8,512]{2,1,0:T(8,128)} all-to-all(f32[32,8,512]{2,1,0:T(8,128)S(1)} %convolution_bitcast_fusion), channel_id=1, replica_groups=mesh['seq'=16,'label'=32] {'label'}, dimensions={0} | all-to-all | bytes 1048576 | tf_op jit(solution)/shard_map/all_to_all | solution.py:130
  37.8 1.8 %shard_map.110 = bf16[32,8,512]{2,1,0:T(8,128)(2,1)} custom-call(f32[32,8,512]{2,1,0:T(8,128)} %all_to_all.35.parts_ref), custom_call_target="tpu_custom_call" | custom-call | tf_op jit(solution)/shard_map/pallas_call | solution.py:151
  39.7 7.5 %all-to-all-start.1 = ((bf16[32,8,512]{2,1,0:T(8,128)(2,1)}), bf16[32,8,512]{2,1,0:T(8,128)(2,1)S(1)}, u32[]{:S(2)}, u32[]{:S(2)}) async-start(bf16[32,8,512]{2,1,0:T(8,128)(2,1)} %shard_map.110), calls=%async_computation.1 | async-start | bytes 524288 | tf_op jit(solution)/shard_map/all_to_all | solution.py:130
  47.1 0.0 reduce-scatter.2.cloned.1.call-start
  47.2 0.8 copy.15.refs_3_
  48.0 8.8 %all-to-all-done.1 = bf16[32,8,512]{2,1,0:T(8,128)(2,1)S(1)} async-done(((bf16[32,8,512]{2,1,0:T(8,128)(2,1)}), bf16[32,8,512]{2,1,0:T(8,128)(2,1)S(1)}, u32[]{:S(2)}, u32[]{:S(2)}) %all-to-all-start.1) | async-done | bytes 262176 | tf_op jit(solution)/shard_map/all_to_all | solution.py:130
  56.8 1.9 %all-gather.3.cloned.1.call-done = bf16[32,32,1024]{2,1,0:T(8,128)(2,1)} async-done(((bf16[2,32,1024]{2,1,0:T(8,128)(2,1)}), bf16[32,32,1024]{2,1,0:T(8,128)(2,1)}) %all-gather.3.cloned.1.call-update) | async-done | bytes 2097168 | tf_op jit(solution)/shard_map/all_gather | solution.py:148
  58.7 0.0 copy-start.1
  58.7 1.6 copy-done.1
  60.3 3.0 %shard_map.111 = f32[16,8,1024]{2,1,0:T(8,128)S(1)} custom-call(bf16[256,512]{1,0:T(8,128)(2,1)S(1)} %bitcast.33, bf16[16,2,32,1024]{3,2,1,0:T(8,128)(2,1)S(1)} %bitcast.29, bf16[16,2,32,1024]{3,2,1,0:T(8,128)(2,1)S(1)} %bitcast.30, s32[256,1]{1,0:T(8,128)S(1)} %copy.15.refs_3_), custom_call_target="tpu_custom_call" | custom-call | tf_op jit(solution)/shard_map/pallas_call | solution.py:168
  63.3 26.0 %all_to_all.36.refs_4_ = f32[16,8,1024]{2,1,0:T(8,128)S(1)} all-to-all(f32[16,8,1024]{2,1,0:T(8,128)S(1)} %shard_map.111), channel_id=1, replica_groups=mesh['seq'=16,'label'=32] {'seq'}, dimensions={0} | all-to-all | bytes 1048576 | tf_op jit(solution)/shard_map/all_to_all | solution.py:130
  89.3 0.0 copy-done.2
  89.3 0.0 copy-done.3
  89.4 0.0 copy-start.5
  89.4 5.0 %shard_map.112 = (f32[4,1024]{1,0:T(4,128)}, f32[1,1024]{1,0:T(1,128)}, f32[16,2,32,1024]{3,2,1,0:T(8,128)}, bf16[256,512]{1,0:T(8,128)(2,1)}) custom-call(bf16[256,512]{1,0:T(8,128)(2,1)S(1)} %bitcast.34, bf16[16,2,32,1024]{3,2,1,0:T(8,128)(2,1)S(1)} %bitcast.31, bf16[16,2,32,1024]{3,2,1,0:T(8,128)(2,1)S(1)} %bitcast.32, s32[256,1]{1,0:T(8,128)S(1)} %copy.15.refs_3_, ...), custom_call_target="tpu_custom_call" | custom-call | tf_op jit(solution)/shard_map/pallas_call | solution.py:178
  94.3 0.0 reduce-scatter.2.cloned.1.call-update
  94.4 5.6 %all-to-all-start.3 = ((bf16[32,8,512]{2,1,0:T(8,128)(2,1)}), bf16[32,8,512]{2,1,0:T(8,128)(2,1)S(1)}, u32[]{:S(2)}, u32[]{:S(2)}) async-start(bf16[32,8,512]{2,1,0:T(8,128)(2,1)} %bitcast.10), calls=%async_computation.4 | async-start | bytes 524288 | tf_op jit(solution)/shard_map/all_to_all | solution.py:130
  100.0 1.3 slice_bitcast_fusion.2.keys_ref
  101.3 10.0 %all-to-all-done.3.parts_ref = bf16[32,8,512]{2,1,0:T(8,128)(2,1)S(1)} async-done(((bf16[32,8,512]{2,1,0:T(8,128)(2,1)}), bf16[32,8,512]{2,1,0:T(8,128)(2,1)S(1)}, u32[]{:S(2)}, u32[]{:S(2)}) %all-to-all-start.3) | async-done | bytes 262176 | tf_op jit(solution)/shard_map/all_to_all | solution.py:130
  111.3 0.0 copy-start.4
  111.3 0.7 copy-done.4
  112.0 1.7 %shard_map.113 = bf16[32,8,512]{2,1,0:T(8,128)(2,1)} custom-call(bf16[32,8,512]{2,1,0:T(8,128)(2,1)} %copy-done.4, bf16[8,512]{1,0:T(8,128)(2,1)} %slice_bitcast_fusion.2.keys_ref), custom_call_target="tpu_custom_call" | custom-call | tf_op jit(solution)/shard_map/pallas_call | solution.py:209
  113.7 14.8 %all_to_all.37 = bf16[32,8,512]{2,1,0:T(8,128)(2,1)S(1)} all-to-all(bf16[32,8,512]{2,1,0:T(8,128)(2,1)} %shard_map.113), channel_id=1, replica_groups=mesh['seq'=16,'label'=32] {'label'}, dimensions={0} | all-to-all | bytes 524288 | tf_op jit(solution)/shard_map/all_to_all | solution.py:130
  128.5 0.0 copy-done.5
  128.5 0.2 fusion
  128.7 16.7 %all_to_all.38.parts_ref = bf16[16,8,512]{2,1,0:T(8,128)(2,1)} all-to-all(bf16[16,8,512]{2,1,0:T(8,128)(2,1)S(1)} %fusion), channel_id=1, replica_groups=mesh['seq'=16,'label'=32] {'seq'}, dimensions={0} | all-to-all | bytes 262144 | tf_op jit(solution)/shard_map/all_to_all | solution.py:130
  145.4 1.6 shard_map.114
  147.0 12.7 %all_to_all.39 = bf16[16,8,512]{2,1,0:T(8,128)(2,1)S(1)} all-to-all(bf16[16,8,512]{2,1,0:T(8,128)(2,1)} %shard_map.114), channel_id=1, replica_groups=mesh['seq'=16,'label'=32] {'seq'}, dimensions={0} | all-to-all | bytes 262144 | tf_op jit(solution)/shard_map/all_to_all | solution.py:130
  159.7 0.7 bitcast_convert_fusion
  160.4 0.0 reduce-scatter.2.cloned.1.call-done
  160.4 1.7 slice_bitcast_fusion
Async XLA Ops:
  7.2 1.7 copy-start
  7.2 51.5 %all-gather.3.cloned.1.call-start = ((), (), s32[]{:S(2)}) async-start(), calls=%async_computation.9 | async-start | bytes 2228224 | tf_op jit(solution)/shard_map/all_gather | solution.py:148
  9.9 79.5 %copy-start.2 = (s32[4,1024]{1,0:T(4,128)S(1)}, s32[4,1024]{1,0:T(4,128)}, u32[]{:S(2)}) copy-start(s32[4,1024]{1,0:T(4,128)} %refs_6_.1) | copy-start | bytes 49156
  9.9 79.5 %copy-start.3 = (f32[1024]{0:T(1024)S(1)}, f32[1024]{0:T(1024)}, u32[]{:S(2)}) copy-start(f32[1024]{0:T(1024)} %param.11) | copy-start | bytes 12292
  39.7 17.1 %all-to-all-start.1 = ((bf16[32,8,512]{2,1,0:T(8,128)(2,1)}), bf16[32,8,512]{2,1,0:T(8,128)(2,1)S(1)}, u32[]{:S(2)}, u32[]{:S(2)}) async-start(bf16[32,8,512]{2,1,0:T(8,128)(2,1)} %shard_map.110), calls=%async_computation.1 | async-start | bytes 524288 | tf_op jit(solution)/shard_map/all_to_all | solution.py:130
  47.1 113.3 %reduce-scatter.2.cloned.1.call-start = ((), (), s32[]{:S(2)}) async-start(), calls=%async_computation.8 | async-start | bytes 4456448 | tf_op jit(solution)/shard_map/reduce_scatter | solution.py:205
  58.7 1.6 copy-start.1
  89.4 39.1 %copy-start.5 = (bf16[256,128]{1,0:T(8,128)(2,1)S(1)}, bf16[256,128]{1,0:T(8,128)(2,1)}, u32[]{:S(2)}) copy-start(bf16[256,128]{1,0:T(8,128)(2,1)} %param.7) | copy-start | bytes 196612
  94.4 16.9 %all-to-all-start.3 = ((bf16[32,8,512]{2,1,0:T(8,128)(2,1)}), bf16[32,8,512]{2,1,0:T(8,128)(2,1)S(1)}, u32[]{:S(2)}, u32[]{:S(2)}) async-start(bf16[32,8,512]{2,1,0:T(8,128)(2,1)} %bitcast.10), calls=%async_computation.4 | async-start | bytes 524288 | tf_op jit(solution)/shard_map/all_to_all | solution.py:130
  111.3 0.7 copy-start.4
Sparse Core Ops, SparseCore 0:
  10.7 47.9 all-gather.2
  94.5 58.2 reduce-scatter.1

commit v2 on v1

v2 whole, which is shorter than its diff:
```python
import jax
import jax.numpy as jnp
from jax import lax
from jax.experimental import pallas as pl
from jax.experimental.pallas import tpu as pltpu
from jax.sharding import PartitionSpec as P

FAR = -1e30
ROWS = (((0,), (0,)), ((), ()))
COLS = (((1,), (1,)), ((), ()))
SPAN = 512
LANES = 128
TAIL = 8


def fetch(vectors_ref, held_ref, sems):
    blocks = []
    for low in range(0, held_ref.shape[-1], SPAN):
        codes = slice(low, low + SPAN)
        copy = pltpu.make_async_copy(
            vectors_ref.at[:, :, :, codes], held_ref.at[:, :, :, codes], sems.at[low // SPAN]
        )
        copy.start()
        blocks.append((codes, copy))
    return blocks


def products(keys, held_ref, codes):
    query_blk = held_ref[:, 0, :, codes].reshape(-1, SPAN)
    output_blk = held_ref[:, 1, :, codes].reshape(-1, SPAN)
    score_vals = jnp.dot(keys, query_blk, preferred_element_type=jnp.float32)
    value_vals = jnp.dot(keys, output_blk, preferred_element_type=jnp.float32)
    return score_vals, value_vals, query_blk, output_blk


def spread(masks, rows):
    spread_vals = rows[-1]
    for mask, row in zip(masks[:-1], rows[:-1]):
        spread_vals = jnp.where(mask, row, spread_vals)
    return spread_vals


def pick(wanted, rows):
    return spread([wanted == rec for rec in range(len(rows))], rows)


def totals_kernel(
    records,
    keys_ref,
    vectors_ref,
    ids_ref,
    own_ref,
    out_ref,
    held_ref,
    sems,
):
    blocks = fetch(vectors_ref, held_ref, sems)
    keys = keys_ref[...]
    ids = ids_ref[...]
    masks = [ids == rec for rec in range(records)]
    first, last = ids[:1], ids[-1:]
    single = first == last
    width = own_ref.shape[1]
    for codes, copy in blocks:
        copy.wait()
        score_vals, value_vals, _, _ = products(keys, held_ref, codes)
        tops = [
            jnp.max(jnp.where(mask, score_vals, FAR), axis=0, keepdims=True) for mask in masks
        ]
        expo = jnp.exp(score_vals - spread(masks, tops))
        weighted = expo * value_vals
        logs, means = [], []
        for mask, top in zip(masks, tops):
            denom = jnp.sum(jnp.where(mask, expo, 0.0), axis=0, keepdims=True)
            numer = jnp.sum(jnp.where(mask, weighted, 0.0), axis=0, keepdims=True)
            some = denom > 0.0
            safe = jnp.where(some, denom, 1.0)
            logs.append(jnp.where(some, top + jnp.log(safe), FAR))
            means.append(jnp.where(some, numer / safe, 0.0))
        own_ref[:, codes] = jnp.concatenate(logs + means, axis=0)
        table = jnp.concatenate(
            [
                pick(first, logs),
                jnp.where(single, FAR, pick(last, logs)),
                pick(first, means),
                jnp.where(single, 0.0, pick(last, means)),
            ],
            axis=0,
        )
        out_ref[:, :, codes] = jnp.broadcast_to(table[None], (out_ref.shape[0], *table.shape))
    marks = jnp.concatenate([first, last, first, last], axis=0).astype(jnp.float32)
    out_ref[:, :, width:] = jnp.broadcast_to(marks[None], (*out_ref.shape[:2], LANES))


def grads_kernel(
    records,
    keys_ref,
    vectors_ref,
    ids_ref,
    own_ref,
    totals_ref,
    leader_ref,
    bias_ref,
    labels_ref,
    grads_ref,
    key_grad_ref,
    held_ref,
    ready_ref,
    sems,
    out_sems,
):
    blocks = fetch(vectors_ref, held_ref, sems)
    keys = keys_ref[...]
    turned = keys.T
    ids = ids_ref[...]
    first, last = ids[:1], ids[-1:]
    masks = [ids == rec for rec in range(records)]
    width = own_ref.shape[1]
    parts = ready_ref.shape[0]
    rows = keys.shape[1] // parts
    widen = lambda lanes: jnp.concatenate([lanes] * (width // LANES), axis=1)
    first_marks = widen(totals_ref[:, 0, width:])
    last_marks = widen(totals_ref[:, 1, width:])
    first_logs, last_logs = totals_ref[:, 0, :width], totals_ref[:, 1, :width]
    first_means, last_means = totals_ref[:, 2, :width], totals_ref[:, 3, :width]
    logs, pools, shows = [], [], []
    for rec in range(records):
        head_logs = jnp.where(first_marks == rec, first_logs, FAR)
        tail_logs = jnp.where(last_marks == rec, last_logs, FAR)
        top = jnp.max(jnp.maximum(head_logs, tail_logs), axis=0, keepdims=True)
        head_weights, tail_weights = jnp.exp(head_logs - top), jnp.exp(tail_logs - top)
        denom = jnp.sum(head_weights + tail_weights, axis=0, keepdims=True)
        numer = jnp.sum(
            head_weights * first_means + tail_weights * last_means, axis=0, keepdims=True
        )
        inner = jnp.logical_and(first < rec, last > rec)
        own_log = own_ref[rec : rec + 1]
        own_mean = own_ref[records + rec : records + rec + 1]
        logs.append(jnp.where(inner, own_log, top + jnp.log(denom)))
        pools.append(jnp.where(inner, own_mean, numer / denom))
        shows.append(jnp.where(inner, 1.0, jnp.where(top > 0.5 * FAR, leader_ref[...], 0.0)))
    logits = jnp.concatenate(pools, axis=0) + bias_ref[...]
    labels_f = labels_ref[...].astype(jnp.float32)
    small = jnp.exp(-jnp.abs(logits))
    loss = jnp.maximum(logits, 0.0) + jnp.log1p(small) - labels_f * logits
    delta = jnp.where(logits >= 0.0, 1.0, small) / (1.0 + small) - labels_f
    show = jnp.concatenate(shows, axis=0) > 0.5
    shown = jnp.concatenate(
        [
            jnp.where(show, loss, 0.0),
            jnp.sum(jnp.where(show, delta, 0.0), axis=0, keepdims=True),
            jnp.zeros((TAIL - records - 1, width), jnp.float32),
        ],
        axis=0,
    )
    ready_ref[:, 2 * rows :, :] = jnp.broadcast_to(shown[None], (parts, *shown.shape))
    deltas = [delta[rec : rec + 1] for rec in range(records)]
    key_grad = jnp.zeros(keys.shape, jnp.float32)
    sent = []
    for codes, copy in blocks:
        copy.wait()
        score_vals, value_vals, query_blk, output_blk = products(keys, held_ref, codes)
        cut = lambda row_list: [row[:, codes] for row in row_list]
        pool_weight = spread(masks, cut(deltas)) * jnp.exp(score_vals - spread(masks, cut(logs)))
        pool_grad = pool_weight.astype(jnp.bfloat16)
        score_grad = (pool_weight * (value_vals - spread(masks, cut(pools)))).astype(jnp.bfloat16)
        ready_ref[:, :rows, codes] = jnp.dot(
            turned, score_grad, preferred_element_type=jnp.float32
        ).reshape(parts, rows, SPAN)
        ready_ref[:, rows : 2 * rows, codes] = jnp.dot(
            turned, pool_grad, preferred_element_type=jnp.float32
        ).reshape(parts, rows, SPAN)
        sent.append(
            pltpu.make_async_copy(
                ready_ref.at[:, :, codes], grads_ref.at[:, :, codes], out_sems.at[len(sent)]
            )
        )
        sent[-1].start()
        key_grad += lax.dot_general(
            score_grad, query_blk, COLS, preferred_element_type=jnp.float32
        )
        key_grad += lax.dot_general(
            pool_grad, output_blk, COLS, preferred_element_type=jnp.float32
        )
    key_grad_ref[...] = key_grad.astype(key_grad_ref.dtype)
    for copy in sent:
        copy.wait()


def pre_grad_kernel(parts_ref, keys_ref, out_ref):
    keys_f = keys_ref[...].astype(jnp.float32)
    total = jnp.sum(parts_ref[...].astype(jnp.float32), axis=0)
    own = (total * (1.0 - keys_f * keys_f)).astype(out_ref.dtype)
    out_ref[...] = jnp.broadcast_to(own[None], out_ref.shape)


def sum_kernel(parts_ref, out_ref):
    own = jnp.sum(parts_ref[...].astype(jnp.float32), axis=0).astype(out_ref.dtype)
    out_ref[...] = jnp.broadcast_to(own[None], out_ref.shape)


def split_kernel(grads_ref, *refs):
    out_refs, sems = refs[:-1], refs[-1]
    copies, row = [], 0
    for out_ref in out_refs:
        rows = out_ref.shape[0]
        copies.append(
            pltpu.make_async_copy(grads_ref.at[row : row + rows], out_ref, sems.at[len(copies)])
        )
        copies[-1].start()
        row += rows
    for copy in copies:
        copy.wait()


def swap(parts, axis):
    return lax.all_to_all(parts, axis, 0, 0, tiled=True)


def struct(shape, dtype):
    return jax.ShapeDtypeStruct(shape, dtype)


def on_device(
    hidden_states, key_weight, queries, output_weight, code_bias, record_ids, code_labels
):
    f32, bf16 = jnp.float32, jnp.bfloat16
    records, width = code_labels.shape
    seq, label = lax.axis_size("seq"), lax.axis_size("label")
    tokens, feats = hidden_states.shape
    dims = key_weight.shape[1]
    rows = queries.shape[0]
    own_toks, own_feats = tokens // label, feats // seq

    few = pltpu.CompilerParams(vmem_limit_bytes=8 * 1024 * 1024)
    many = pltpu.CompilerParams(vmem_limit_bytes=52 * 1024 * 1024)
    most = pltpu.CompilerParams(vmem_limit_bytes=59 * 1024 * 1024)

    vectors = lax.all_gather(jnp.stack([queries, output_weight]), "seq", axis=0)
    partial_pre = jnp.dot(hidden_states, key_weight, preferred_element_type=f32)
    pre_parts = swap(partial_pre.reshape(label, own_toks, dims), "label")
    keys_own = jnp.tanh(jnp.sum(pre_parts, axis=0)).astype(bf16)
    keys_copies = jnp.broadcast_to(keys_own[None], (label, own_toks, dims))
    keys_all = swap(keys_copies, "label").reshape(tokens, dims)

    ids = record_ids[:, None]
    leader = (lax.axis_index("seq") == 0).astype(f32).reshape(1, 1)
    held = pl.BlockSpec(memory_space=pltpu.VMEM)
    far = pl.BlockSpec(memory_space=pltpu.HBM)
    blocks = width // SPAN
    vector_scratch = pltpu.VMEM((seq, 2, rows, width), bf16)
    own_totals, totals = pl.pallas_call(
        lambda *refs: totals_kernel(records, *refs),
        in_specs=[held, far, held],
        out_specs=[held, held],
        out_shape=[
            struct((2 * records, width), f32),
            struct((seq, 4, width + LANES), f32),
        ],
        scratch_shapes=[vector_scratch, pltpu.SemaphoreType.DMA((blocks,))],
        compiler_params=many,
    )(keys_all, vectors, ids)
    totals = swap(totals, "seq")

    grads, key_grad = pl.pallas_call(
        lambda *refs: grads_kernel(records, *refs),
        in_specs=[held, far, *[held] * 6],
        out_specs=[far, held],
        out_shape=[
            struct((seq, 2 * rows + TAIL, width), f32),
            struct((tokens, dims), bf16),
        ],
        scratch_shapes=[
            vector_scratch,
            pltpu.VMEM((seq, 2 * rows + TAIL, width), f32),
            pltpu.SemaphoreType.DMA((blocks,)),
            pltpu.SemaphoreType.DMA((blocks,)),
        ],
        compiler_params=many,
    )(
        keys_all,
        vectors,
        ids,
        own_totals,
        totals,
        leader,
        code_bias[None],
        code_labels,
    )

    grads = lax.psum_scatter(grads, "seq", scatter_dimension=0)
    grad_queries, grad_output, code_loss, grad_bias = pl.pallas_call(
        split_kernel,
        out_shape=[
            struct((rows, width), f32),
            struct((rows, width), f32),
            struct((records, width), f32),
            struct((1, width), f32),
        ],
        in_specs=[far],
        out_specs=[far] * 4,
        scratch_shapes=[pltpu.SemaphoreType.DMA((4,))],
        compiler_params=most,
    )(grads)

    key_parts = swap(key_grad.reshape(label, own_toks, dims), "label")
    pre_copies = pl.pallas_call(
        pre_grad_kernel, out_shape=struct((label, own_toks, dims), bf16), compiler_params=few
    )(key_parts, keys_own)
    pre_grad = swap(pre_copies, "label").reshape(tokens, dims)
    weight_part = lax.dot_general(
        hidden_states, pre_grad, ROWS, preferred_element_type=f32
    ).astype(bf16)
    weight_parts = swap(weight_part.reshape(seq, own_feats, dims), "seq")
    weight_copies = pl.pallas_call(
        sum_kernel, out_shape=struct((seq, own_feats, dims), bf16), compiler_params=few
    )(weight_parts)
    grad_key_weight = swap(weight_copies, "seq").reshape(feats, dims).astype(f32)
    return (code_loss, grad_queries, grad_output, grad_bias[0], grad_key_weight)


def solution(mesh):
    return jax.shard_map(
        on_device,
        mesh=mesh,
        in_specs=(
            P("seq", "label"),
            P("label", None),
            P("seq", "label"),
            P("seq", "label"),
            P("label"),
            P("seq"),
            P(None, "label"),
        ),
        out_specs=(
            P(None, "label"),
            P("seq", "label"),
            P("seq", "label"),
            P("label"),
            P("label", None),
        ),
        check_vma=False,
    )
```

time: 170 us -> 170 us (level); the launches traced: 169 us -> 167 us
  blocking collectives: 98.2 us -> 88.9 us
  Pallas kernels: 13.1 us -> 19.2 us
  local copies, waits for them, and re-layouts: 6.11 us -> 1.55 us
  waiting for transfers between devices: 20.7 us -> 24.1 us
  starting transfers between devices: 13.1 us -> 15.5 us
    all_to_all x5, blocking collectives: 98.2 us -> 88.9 us  [swap(): return lax.all_to_all(parts, axis, 0, 0, tiled=True)]
    pallas_call x4, Pallas kernels: 11.4 us -> 19.1 us  [the longest x1 9.7 us: on_device(): pl.pallas_call(split_kernel, out_shape=[struct((rows, width), f32), struc...]
    squeeze x2 -> x0, local copies, waits for them, and re-layouts: 2.98 us -> none  [the longest x1 1.68 us: on_device(): grad_queries, grad_output = (grads[0], grads[1])]
    all_to_all x2, waiting for transfers between devices: 18.8 us -> 21.1 us  [swap(): return lax.all_to_all(parts, axis, 0, 0, tiled=True)]
    all_to_all x2, starting transfers between devices: 13.1 us -> 15.4 us  [swap(): return lax.all_to_all(parts, axis, 0, 0, tiled=True)]
    unnamed x12 -> x8, local copies, waits for them, and re-layouts: 2.32 us -> 0.02 us
  transfers between devices with their start and end apart: 4 -> 4, of which waited for: 3 -> 3; matrix products, arithmetic and copies ran while one was open for 2% -> 2% of each run, Pallas kernels for 3% -> 0%
where the time goes in v2:
time: 170 us; the launch traced here: 167 us
  blocking collectives  88.9 us (52%)
  waiting for transfers between devices  24.1 us (14%)
  Pallas kernels  19.2 us (11%)
  starting transfers between devices  15.5 us (9%)
  between operations  14.2 us (8%)
  other arithmetic  2.34 us (1%)
    all_to_all x5, blocking collectives, swap(): return lax.all_to_all(parts, axis, 0, 0, tiled=True)  88.9 us
    all_to_all x2, waiting for transfers between devices, swap(): return lax.all_to_all(parts, axis, 0, 0, tiled=True)  21.1 us
    all_to_all x2, starting transfers between devices, swap(): return lax.all_to_all(parts, axis, 0, 0, tiled=True)  15.4 us
    pallas_call x1, Pallas kernels, on_device(): pl.pallas_call(split_kernel, out_shape=[struct((rows, width), f32), struc...  9.7 us
    pallas_call x1, Pallas kernels, on_device(): pl.pallas_call(lambda *refs: grads_kernel(records, *refs), in_specs=[held...  5.28 us
    pallas_call x1, Pallas kernels, on_device(): pl.pallas_call(lambda *refs: totals_kernel(records, *refs), in_specs=[hel...  4.11 us
  transfers between devices with their start and end apart: 4, of which 3 were waited for; matrix products, arithmetic and copies ran while one was open for 2% of the time, Pallas kernels for 0%

profile of v2, /device:TPU:1, one launch (start us, length us, event | category | flops | bytes accessed | tf_op | source)
XLA Modules:
  0.0 166.9 jit_solution(1654123212704521120)
XLA Ops:
  7.2 0.0 copy-start
  7.2 0.0 copy-start.1
  7.2 0.0 copy-start.2
  7.2 0.0 all-gather.3.cloned.1.call-start
  7.2 1.6 pad_maximum_fusion
  8.8 0.0 all-gather.3.cloned.1.call-update
  8.8 0.0 copy-done
  8.8 1.0 convolution_bitcast_fusion
  9.9 27.8 %all_to_all.35 = f32[32,8,512]{2,1,0:T(8,128)S(1)} all-to-all(f32[32,8,512]{2,1,0:T(8,128)S(1)} %convolution_bitcast_fusion), channel_id=1, replica_groups=mesh['seq'=16,'label'=32] {'label'}, dimensions={0} | all-to-all | bytes 1048576 | tf_op jit(solution)/shard_map/all_to_all | solution.py:217
  37.8 0.7 broadcast_in_dim.12
  38.5 7.5 %all-to-all-start.1 = ((bf16[32,8,512]{2,1,0:T(8,128)(2,1)}), bf16[32,8,512]{2,1,0:T(8,128)(2,1)S(1)}, u32[]{:S(2)}, u32[]{:S(2)}) async-start(bf16[32,8,512]{2,1,0:T(8,128)(2,1)} %broadcast_in_dim.12), calls=%async_computation.1 | async-start | bytes 524288 | tf_op jit(solution)/shard_map/all_to_all | solution.py:217
  46.0 0.8 copy.15.refs_2_
  46.8 8.8 %all-to-all-done.1 = bf16[32,8,512]{2,1,0:T(8,128)(2,1)S(1)} async-done(((bf16[32,8,512]{2,1,0:T(8,128)(2,1)}), bf16[32,8,512]{2,1,0:T(8,128)(2,1)S(1)}, u32[]{:S(2)}, u32[]{:S(2)}) %all-to-all-start.1) | async-done | bytes 262176 | tf_op jit(solution)/shard_map/all_to_all | solution.py:217
  55.7 2.9 %all-gather.3.cloned.1.call-done = bf16[32,32,1024]{2,1,0:T(8,128)(2,1)} async-done(((bf16[2,32,1024]{2,1,0:T(8,128)(2,1)}), bf16[32,32,1024]{2,1,0:T(8,128)(2,1)}) %all-gather.3.cloned.1.call-update) | async-done | bytes 2097168 | tf_op jit(solution)/shard_map/all_gather | solution.py:239
  58.5 4.1 %shard_map.110 = (f32[8,1024]{1,0:T(8,128)S(1)}, f32[16,4,1152]{2,1,0:T(4,128)}) custom-call(bf16[256,512]{1,0:T(8,128)(2,1)S(1)} %bitcast.25, bf16[16,2,32,1024]{3,2,1,0:T(8,128)(2,1)} %bitcast.29, s32[256,1]{1,0:T(8,128)S(1)} %copy.15.refs_2_), custom_call_target="tpu_custom_call" | custom-call | tf_op jit(solution)/shard_map/pallas_call | solution.py:252
  62.7 7.9 %all-to-all-start.2 = ((f32[16,4,1152]{2,1,0:T(4,128)}), f32[16,4,1152]{2,1,0:T(4,128)S(1)}, u32[]{:S(2)}, u32[]{:S(2)}) async-start(f32[16,4,1152]{2,1,0:T(4,128)} %get-tuple-element.14), calls=%async_computation.2 | async-start | bytes 589824 | tf_op jit(solution)/shard_map/all_to_all | solution.py:217
  70.6 0.0 copy-start.3
  70.6 0.0 reduce-scatter.2.cloned.1.call-start
  70.7 12.3 %all-to-all-done.2.refs_4_ = f32[16,4,1152]{2,1,0:T(4,128)S(1)} async-done(((f32[16,4,1152]{2,1,0:T(4,128)}), f32[16,4,1152]{2,1,0:T(4,128)S(1)}, u32[]{:S(2)}, u32[]{:S(2)}) %all-to-all-start.2) | async-done | bytes 294944 | tf_op jit(solution)/shard_map/all_to_all | solution.py:217
  83.0 0.0 copy-done.1
  83.0 0.0 copy-done.2
  83.0 5.3 %shard_map.111 = (f32[16,72,1024]{2,1,0:T(8,128)}, bf16[256,512]{1,0:T(8,128)(2,1)S(1)}) custom-call(bf16[256,512]{1,0:T(8,128)(2,1)S(1)} %bitcast.26, bf16[16,2,32,1024]{3,2,1,0:T(8,128)(2,1)} %bitcast.30, s32[256,1]{1,0:T(8,128)S(1)} %copy.15.refs_2_, f32[8,1024]{1,0:T(8,128)S(1)} %get-tuple-element.13.refs_3_, f32[16,4,1152]{2,1,0:T(4,128)S(1)} %all-to-all-done.2.refs_4_, ...), custom_call_target="tpu_custom_call" | custom-call | tf_op jit(solution)/shard_map/pallas_call | solution.py:265
  88.3 0.0 reduce-scatter.2.cloned.1.call-update
  88.3 17.6 %all_to_all.36.parts_ref = bf16[32,8,512]{2,1,0:T(8,128)(2,1)S(1)} all-to-all(bf16[32,8,512]{2,1,0:T(8,128)(2,1)S(1)} %bitcast.27), channel_id=1, replica_groups=mesh['seq'=16,'label'=32] {'label'}, dimensions={0} | all-to-all | bytes 524288 | tf_op jit(solution)/shard_map/all_to_all | solution.py:217
  105.9 0.1 shard_map.113
  105.9 15.4 %all_to_all.37 = bf16[32,8,512]{2,1,0:T(8,128)(2,1)S(1)} all-to-all(bf16[32,8,512]{2,1,0:T(8,128)(2,1)S(1)} %shard_map.113), channel_id=1, replica_groups=mesh['seq'=16,'label'=32] {'label'}, dimensions={0} | all-to-all | bytes 524288 | tf_op jit(solution)/shard_map/all_to_all | solution.py:217
  121.3 0.0 copy-done.3
  121.3 0.2 fusion
  121.5 14.7 %all_to_all.38.parts_ref = bf16[16,8,512]{2,1,0:T(8,128)(2,1)S(1)} all-to-all(bf16[16,8,512]{2,1,0:T(8,128)(2,1)S(1)} %fusion), channel_id=1, replica_groups=mesh['seq'=16,'label'=32] {'seq'}, dimensions={0} | all-to-all | bytes 262144 | tf_op jit(solution)/shard_map/all_to_all | solution.py:217
  136.3 13.3 %all_to_all.39 = bf16[16,8,512]{2,1,0:T(8,128)(2,1)S(1)} all-to-all(bf16[16,8,512]{2,1,0:T(8,128)(2,1)S(1)} %shard_map.114), channel_id=1, replica_groups=mesh['seq'=16,'label'=32] {'seq'}, dimensions={0} | all-to-all | bytes 262144 | tf_op jit(solution)/shard_map/all_to_all | solution.py:217
  149.6 0.7 bitcast_convert_fusion
  150.4 0.0 reduce-scatter.2.cloned.1.call-done
  150.4 9.7 %shard_map.112 = (f32[32,1024]{1,0:T(8,128)}, f32[32,1024]{1,0:T(8,128)}, f32[4,1024]{1,0:T(4,128)}, f32[1,1024]{1,0:T(1,128)}) custom-call(f32[72,1024]{1,0:T(8,128)} %bitcast.31), custom_call_target="tpu_custom_call" | custom-call | tf_op jit(solution)/shard_map/pallas_call | solution.py:292
  (3 shorter events, 0.1 us)
Async XLA Ops:
  7.2 1.7 copy-start
  7.2 75.8 %copy-start.1 = (s32[4,1024]{1,0:T(4,128)S(1)}, s32[4,1024]{1,0:T(4,128)}, u32[]{:S(2)}) copy-start(s32[4,1024]{1,0:T(4,128)} %refs_7_.1) | copy-start | bytes 49156
  7.2 75.8 %copy-start.2 = (f32[1024]{0:T(1024)S(1)}, f32[1024]{0:T(1024)}, u32[]{:S(2)}) copy-start(f32[1024]{0:T(1024)} %param.11) | copy-start | bytes 12292
  7.2 51.3 %all-gather.3.cloned.1.call-start = ((), (), s32[]{:S(2)}) async-start(), calls=%async_computation.9 | async-start | bytes 2228224 | tf_op jit(solution)/shard_map/all_gather | solution.py:239
  38.5 17.1 %all-to-all-start.1 = ((bf16[32,8,512]{2,1,0:T(8,128)(2,1)}), bf16[32,8,512]{2,1,0:T(8,128)(2,1)S(1)}, u32[]{:S(2)}, u32[]{:S(2)}) async-start(bf16[32,8,512]{2,1,0:T(8,128)(2,1)} %broadcast_in_dim.12), calls=%async_computation.1 | async-start | bytes 524288 | tf_op jit(solution)/shard_map/all_to_all | solution.py:217
  62.7 20.3 %all-to-all-start.2 = ((f32[16,4,1152]{2,1,0:T(4,128)}), f32[16,4,1152]{2,1,0:T(4,128)S(1)}, u32[]{:S(2)}, u32[]{:S(2)}) async-start(f32[16,4,1152]{2,1,0:T(4,128)} %get-tuple-element.14), calls=%async_computation.2 | async-start | bytes 589824 | tf_op jit(solution)/shard_map/all_to_all | solution.py:217
  70.6 50.7 %copy-start.3 = (bf16[256,128]{1,0:T(8,128)(2,1)S(1)}, bf16[256,128]{1,0:T(8,128)(2,1)}, u32[]{:S(2)}) copy-start(bf16[256,128]{1,0:T(8,128)(2,1)} %param.7) | copy-start | bytes 196612
  70.6 79.8 %reduce-scatter.2.cloned.1.call-start = ((), (), s32[]{:S(2)}) async-start(), calls=%async_computation.8 | async-start | bytes 5013504 | tf_op jit(solution)/shard_map/reduce_scatter | solution.py:291
Sparse Core Ops, SparseCore 0:
  10.7 47.7 all-gather.2
  88.4 61.7 reduce-scatter.1

commit v3 on v2

--- a/solution.py
+++ b/solution.py
@@ -10,7 +10,6 @@
 COLS = (((1,), (1,)), ((), ()))
 SPAN = 512
 LANES = 128
-TAIL = 8
 
 
 def fetch(vectors_ref, held_ref, sems):
@@ -92,6 +91,11 @@
     out_ref[:, :, width:] = jnp.broadcast_to(marks[None], (*out_ref.shape[:2], LANES))
 
 
+def halves(vals):
+    high = vals.astype(jnp.bfloat16).astype(jnp.float32)
+    return high, vals - high
+
+
 def grads_kernel(
     records,
     keys_ref,
@@ -145,14 +149,8 @@
     loss = jnp.maximum(logits, 0.0) + jnp.log1p(small) - labels_f * logits
     delta = jnp.where(logits >= 0.0, 1.0, small) / (1.0 + small) - labels_f
     show = jnp.concatenate(shows, axis=0) > 0.5
-    shown = jnp.concatenate(
-        [
-            jnp.where(show, loss, 0.0),
-            jnp.sum(jnp.where(show, delta, 0.0), axis=0, keepdims=True),
-            jnp.zeros((TAIL - records - 1, width), jnp.float32),
-        ],
-        axis=0,
-    )
+    shown = [*halves(jnp.where(show, loss, 0.0)), *halves(jnp.where(show, delta, 0.0))]
+    shown = jnp.concatenate(shown, axis=0).astype(ready_ref.dtype)
     ready_ref[:, 2 * rows :, :] = jnp.broadcast_to(shown[None], (parts, *shown.shape))
     deltas = [delta[rec : rec + 1] for rec in range(records)]
     key_grad = jnp.zeros(keys.shape, jnp.float32)
@@ -164,12 +162,11 @@
         pool_weight = spread(masks, cut(deltas)) * jnp.exp(score_vals - spread(masks, cut(logs)))
         pool_grad = pool_weight.astype(jnp.bfloat16)
         score_grad = (pool_weight * (value_vals - spread(masks, cut(pools)))).astype(jnp.bfloat16)
-        ready_ref[:, :rows, codes] = jnp.dot(
-            turned, score_grad, preferred_element_type=jnp.float32
-        ).reshape(parts, rows, SPAN)
-        ready_ref[:, rows : 2 * rows, codes] = jnp.dot(
-            turned, pool_grad, preferred_element_type=jnp.float32
-        ).reshape(parts, rows, SPAN)
+        for half, grad in enumerate((score_grad, pool_grad)):
+            sums = jnp.dot(turned, grad, preferred_element_type=jnp.float32)
+            ready_ref[:, half * rows : (half + 1) * rows, codes] = sums.astype(
+                ready_ref.dtype
+            ).reshape(parts, rows, SPAN)
         sent.append(
             pltpu.make_async_copy(
                 ready_ref.at[:, :, codes], grads_ref.at[:, :, codes], out_sems.at[len(sent)]
@@ -199,18 +196,16 @@
     out_ref[...] = jnp.broadcast_to(own[None], out_ref.shape)
 
 
-def split_kernel(grads_ref, *refs):
-    out_refs, sems = refs[:-1], refs[-1]
-    copies, row = [], 0
-    for out_ref in out_refs:
-        rows = out_ref.shape[0]
-        copies.append(
-            pltpu.make_async_copy(grads_ref.at[row : row + rows], out_ref, sems.at[len(copies)])
-        )
-        copies[-1].start()
-        row += rows
-    for copy in copies:
-        copy.wait()
+def final_kernel(
+    grads_ref, weight_ref, loss_ref, grad_query_ref, grad_output_ref, grad_bias_ref, out_ref
+):
+    rows, records = grad_query_ref.shape[0], loss_ref.shape[0]
+    grad_query_ref[...] = grads_ref[:rows].astype(jnp.float32)
+    grad_output_ref[...] = grads_ref[rows : 2 * rows].astype(jnp.float32)
+    shown = grads_ref[2 * rows :].astype(jnp.float32)
+    loss_ref[...] = shown[:records] + shown[records : 2 * records]
+    grad_bias_ref[...] = jnp.sum(shown[2 * records :], axis=0, keepdims=True)
+    out_ref[...] = weight_ref[...].astype(jnp.float32)
 
 
 def swap(parts, axis):
@@ -234,7 +229,6 @@
 
     few = pltpu.CompilerParams(vmem_limit_bytes=8 * 1024 * 1024)
     many = pltpu.CompilerParams(vmem_limit_bytes=52 * 1024 * 1024)
-    most = pltpu.CompilerParams(vmem_limit_bytes=59 * 1024 * 1024)
 
     vectors = lax.all_gather(jnp.stack([queries, output_weight]), "seq", axis=0)
     partial_pre = jnp.dot(hidden_states, key_weight, preferred_element_type=f32)
@@ -267,12 +261,12 @@
         in_specs=[held, far, *[held] * 6],
         out_specs=[far, held],
         out_shape=[
-            struct((seq, 2 * rows + TAIL, width), f32),
+            struct((seq, 2 * rows + 4 * records, width), bf16),
             struct((tokens, dims), bf16),
         ],
         scratch_shapes=[
             vector_scratch,
-            pltpu.VMEM((seq, 2 * rows + TAIL, width), f32),
+            pltpu.VMEM((seq, 2 * rows + 4 * records, width), bf16),
             pltpu.SemaphoreType.DMA((blocks,)),
             pltpu.SemaphoreType.DMA((blocks,)),
         ],
@@ -289,19 +283,6 @@
     )
 
     grads = lax.psum_scatter(grads, "seq", scatter_dimension=0)
-    grad_queries, grad_output, code_loss, grad_bias = pl.pallas_call(
-        split_kernel,
-        out_shape=[
-            struct((rows, width), f32),
-            struct((rows, width), f32),
-            struct((records, width), f32),
-            struct((1, width), f32),
-        ],
-        in_specs=[far],
-        out_specs=[far] * 4,
-        scratch_shapes=[pltpu.SemaphoreType.DMA((4,))],
-        compiler_params=most,
-    )(grads)
 
     key_parts = swap(key_grad.reshape(label, own_toks, dims), "label")
     pre_copies = pl.pallas_call(
@@ -315,7 +296,20 @@
     weight_copies = pl.pallas_call(
         sum_kernel, out_shape=struct((seq, own_feats, dims), bf16), compiler_params=few
     )(weight_parts)
-    grad_key_weight = swap(weight_copies, "seq").reshape(feats, dims).astype(f32)
+    weights = swap(weight_copies, "seq").reshape(feats, dims)
+    code_loss, grad_queries, grad_output, grad_bias, grad_key_weight = pl.pallas_call(
+        final_kernel,
+        out_shape=[
+            struct((records, width), f32),
+            struct((rows, width), f32),
+            struct((rows, width), f32),
+            struct((1, width), f32),
+            struct((feats, dims), f32),
+        ],
+        in_specs=[held, held],
+        out_specs=[held] * 5,
+        compiler_params=many,
+    )(grads, weights)
     return (code_loss, grad_queries, grad_output, grad_bias[0], grad_key_weight)
 
 

time: 170 us -> 158 us (0.929); the launches traced: 167 us -> 157 us
  Pallas kernels: 19.2 us -> 9.99 us
    pallas_call x1, Pallas kernels: 9.7 us -> 0.81 us  [on_device(): pl.pallas_call(final_kernel, out_shape=[struct((records, width), f32), st...]
  transfers between devices with their start and end apart: 4 -> 4, of which waited for: 3 -> 3; matrix products, arithmetic and copies ran while one was open for 2% -> 1% of each run, Pallas kernels for 0% -> 0%
where the time goes in v3:
time: 158 us; the launch traced here: 157 us
  blocking collectives  88.2 us (56%)
  waiting for transfers between devices  24.7 us (16%)
  starting transfers between devices  15.5 us (10%)
  between operations  14.2 us (9%)
  Pallas kernels  9.99 us (6%)
  local copies, waits for them, and re-layouts  1.8 us (1%)
  other arithmetic  1.61 us (1%)
    all_to_all x5, blocking collectives, swap(): return lax.all_to_all(parts, axis, 0, 0, tiled=True)  88.2 us
    all_to_all x2, waiting for transfers between devices, swap(): return lax.all_to_all(parts, axis, 0, 0, tiled=True)  21.8 us
    all_to_all x2, starting transfers between devices, swap(): return lax.all_to_all(parts, axis, 0, 0, tiled=True)  15.4 us
    pallas_call x1, Pallas kernels, on_device(): pl.pallas_call(lambda *refs: grads_kernel(records, *refs), in_specs=[held...  4.98 us
    pallas_call x1, Pallas kernels, on_device(): pl.pallas_call(lambda *refs: totals_kernel(records, *refs), in_specs=[hel...  4.12 us
  transfers between devices with their start and end apart: 4, of which 3 were waited for; matrix products, arithmetic and copies ran while one was open for 1% of the time, Pallas kernels for 0%

profile of v3, /device:TPU:1, one launch (start us, length us, event | category | flops | bytes accessed | tf_op | source)
XLA Modules:
  0.0 157.3 jit_solution(12111919334317883132)
XLA Ops:
  7.2 0.0 copy-start
  7.2 0.0 copy-start.5
  7.2 0.0 all-gather.3.cloned.1.call-start
  7.2 1.6 pad_maximum_fusion
  8.8 0.0 all-gather.3.cloned.1.call-update
  8.8 0.0 copy-done
  8.8 1.0 convolution_bitcast_fusion
  9.9 0.0 copy-start.2
  9.9 0.0 copy-start.3
  9.9 27.8 %all_to_all.35 = f32[32,8,512]{2,1,0:T(8,128)S(1)} all-to-all(f32[32,8,512]{2,1,0:T(8,128)S(1)} %convolution_bitcast_fusion), channel_id=1, replica_groups=mesh['seq'=16,'label'=32] {'label'}, dimensions={0} | all-to-all | bytes 1048576 | tf_op jit(solution)/shard_map/all_to_all | solution.py:212
  37.8 0.7 broadcast_in_dim.12
  38.5 7.5 %all-to-all-start.1 = ((bf16[32,8,512]{2,1,0:T(8,128)(2,1)}), bf16[32,8,512]{2,1,0:T(8,128)(2,1)S(1)}, u32[]{:S(2)}, u32[]{:S(2)}) async-start(bf16[32,8,512]{2,1,0:T(8,128)(2,1)} %broadcast_in_dim.12), calls=%async_computation.1 | async-start | bytes 524288 | tf_op jit(solution)/shard_map/all_to_all | solution.py:212
  46.0 0.0 copy-done.5
  46.0 0.1 copy.15.refs_2_
  46.2 9.5 %all-to-all-done.1 = bf16[32,8,512]{2,1,0:T(8,128)(2,1)S(1)} async-done(((bf16[32,8,512]{2,1,0:T(8,128)(2,1)}), bf16[32,8,512]{2,1,0:T(8,128)(2,1)S(1)}, u32[]{:S(2)}, u32[]{:S(2)}) %all-to-all-start.1) | async-done | bytes 262176 | tf_op jit(solution)/shard_map/all_to_all | solution.py:212
  55.7 2.9 %all-gather.3.cloned.1.call-done = bf16[32,32,1024]{2,1,0:T(8,128)(2,1)} async-done(((bf16[2,32,1024]{2,1,0:T(8,128)(2,1)}), bf16[32,32,1024]{2,1,0:T(8,128)(2,1)}) %all-gather.3.cloned.1.call-update) | async-done | bytes 2097168 | tf_op jit(solution)/shard_map/all_gather | solution.py:233
  58.5 4.1 %shard_map.110 = (f32[8,1024]{1,0:T(8,128)S(1)}, f32[16,4,1152]{2,1,0:T(4,128)}) custom-call(bf16[256,512]{1,0:T(8,128)(2,1)S(1)} %bitcast.23, bf16[16,2,32,1024]{3,2,1,0:T(8,128)(2,1)} %bitcast.29, s32[256,1]{1,0:T(8,128)S(1)} %copy.15.refs_2_), custom_call_target="tpu_custom_call" | custom-call | tf_op jit(solution)/shard_map/pallas_call | solution.py:246
  62.7 7.9 %all-to-all-start.2 = ((f32[16,4,1152]{2,1,0:T(4,128)}), f32[16,4,1152]{2,1,0:T(4,128)S(1)}, u32[]{:S(2)}, u32[]{:S(2)}) async-start(f32[16,4,1152]{2,1,0:T(4,128)} %get-tuple-element.15), calls=%async_computation.2 | async-start | bytes 589824 | tf_op jit(solution)/shard_map/all_to_all | solution.py:212
  70.6 0.0 reduce-scatter.2.cloned.1.call-start
  70.7 12.3 %all-to-all-done.2.refs_4_ = f32[16,4,1152]{2,1,0:T(4,128)S(1)} async-done(((f32[16,4,1152]{2,1,0:T(4,128)}), f32[16,4,1152]{2,1,0:T(4,128)S(1)}, u32[]{:S(2)}, u32[]{:S(2)}) %all-to-all-start.2) | async-done | bytes 294944 | tf_op jit(solution)/shard_map/all_to_all | solution.py:212
  83.0 0.0 copy-done.2
  83.0 0.0 copy-done.3
  83.0 5.0 %shard_map.111 = (bf16[16,80,1024]{2,1,0:T(8,128)(2,1)}, bf16[256,512]{1,0:T(8,128)(2,1)S(1)}) custom-call(bf16[256,512]{1,0:T(8,128)(2,1)S(1)} %bitcast.24, bf16[16,2,32,1024]{3,2,1,0:T(8,128)(2,1)} %bitcast.30, s32[256,1]{1,0:T(8,128)S(1)} %copy.15.refs_2_, f32[8,1024]{1,0:T(8,128)S(1)} %get-tuple-element.14.refs_3_, ...), custom_call_target="tpu_custom_call" | custom-call | tf_op jit(solution)/shard_map/pallas_call | solution.py:259
  88.0 0.0 copy-start.4
  88.0 0.0 reduce-scatter.2.cloned.1.call-update
  88.0 17.6 %all_to_all.36.parts_ref = bf16[32,8,512]{2,1,0:T(8,128)(2,1)S(1)} all-to-all(bf16[32,8,512]{2,1,0:T(8,128)(2,1)S(1)} %bitcast.26), channel_id=1, replica_groups=mesh['seq'=16,'label'=32] {'label'}, dimensions={0} | all-to-all | bytes 524288 | tf_op jit(solution)/shard_map/all_to_all | solution.py:212
  105.6 0.1 shard_map.112
  105.6 15.4 %all_to_all.37 = bf16[32,8,512]{2,1,0:T(8,128)(2,1)S(1)} all-to-all(bf16[32,8,512]{2,1,0:T(8,128)(2,1)S(1)} %shard_map.112), channel_id=1, replica_groups=mesh['seq'=16,'label'=32] {'label'}, dimensions={0} | all-to-all | bytes 524288 | tf_op jit(solution)/shard_map/all_to_all | solution.py:212
  121.0 0.0 copy-done.4
  121.0 0.2 fusion
  121.2 16.0 %all_to_all.38.parts_ref = bf16[16,8,512]{2,1,0:T(8,128)(2,1)S(1)} all-to-all(bf16[16,8,512]{2,1,0:T(8,128)(2,1)S(1)} %fusion), channel_id=1, replica_groups=mesh['seq'=16,'label'=32] {'seq'}, dimensions={0} | all-to-all | bytes 262144 | tf_op jit(solution)/shard_map/all_to_all | solution.py:212
  137.3 11.4 %all_to_all.39 = bf16[16,8,512]{2,1,0:T(8,128)(2,1)S(1)} all-to-all(bf16[16,8,512]{2,1,0:T(8,128)(2,1)S(1)} %shard_map.113), channel_id=1, replica_groups=mesh['seq'=16,'label'=32] {'seq'}, dimensions={0} | all-to-all | bytes 262144 | tf_op jit(solution)/shard_map/all_to_all | solution.py:212
  148.7 0.0 reduce-scatter.2.cloned.1.call-done
  148.7 0.0 copy-start.1
  148.7 0.9 copy-done.1
  149.6 0.8 shard_map.114
  (3 shorter events, 0.1 us)
Async XLA Ops:
  7.2 1.6 %copy-start = (bf16[128,512]{1,0:T(8,128)(2,1)S(1)}, bf16[128,512]{1,0:T(8,128)(2,1)}, u32[]{:S(2)}) copy-start(bf16[128,512]{1,0:T(8,128)(2,1)} %param.8) | copy-start | bytes 393220
  7.2 38.8 %copy-start.5 = (s32[256]{0:T(256)S(1)}, s32[256]{0:T(256)}, u32[]{:S(2)}) copy-start(s32[256]{0:T(256)} %param.12) | copy-start | bytes 3076
  7.2 51.3 %all-gather.3.cloned.1.call-start = ((), (), s32[]{:S(2)}) async-start(), calls=%async_computation.9 | async-start | bytes 2228224 | tf_op jit(solution)/shard_map/all_gather | solution.py:233
  9.9 73.1 %copy-start.2 = (s32[4,1024]{1,0:T(4,128)S(1)}, s32[4,1024]{1,0:T(4,128)}, u32[]{:S(2)}) copy-start(s32[4,1024]{1,0:T(4,128)} %refs_7_.1) | copy-start | bytes 49156
  9.9 73.1 %copy-start.3 = (f32[1024]{0:T(1024)S(1)}, f32[1024]{0:T(1024)}, u32[]{:S(2)}) copy-start(f32[1024]{0:T(1024)} %param.11) | copy-start | bytes 12292
  38.5 17.1 %all-to-all-start.1 = ((bf16[32,8,512]{2,1,0:T(8,128)(2,1)}), bf16[32,8,512]{2,1,0:T(8,128)(2,1)S(1)}, u32[]{:S(2)}, u32[]{:S(2)}) async-start(bf16[32,8,512]{2,1,0:T(8,128)(2,1)} %broadcast_in_dim.12), calls=%async_computation.1 | async-start | bytes 524288 | tf_op jit(solution)/shard_map/all_to_all | solution.py:212
  62.7 20.3 %all-to-all-start.2 = ((f32[16,4,1152]{2,1,0:T(4,128)}), f32[16,4,1152]{2,1,0:T(4,128)S(1)}, u32[]{:S(2)}, u32[]{:S(2)}) async-start(f32[16,4,1152]{2,1,0:T(4,128)} %get-tuple-element.15), calls=%async_computation.2 | async-start | bytes 589824 | tf_op jit(solution)/shard_map/all_to_all | solution.py:212
  70.6 78.1 %reduce-scatter.2.cloned.1.call-start = ((), (), s32[]{:S(2)}) async-start(), calls=%async_computation.8 | async-start | bytes 2785280 | tf_op jit(solution)/shard_map/reduce_scatter | solution.py:285
  88.0 33.0 %copy-start.4 = (bf16[256,128]{1,0:T(8,128)(2,1)S(1)}, bf16[256,128]{1,0:T(8,128)(2,1)}, u32[]{:S(2)}) copy-start(bf16[256,128]{1,0:T(8,128)(2,1)} %param.7) | copy-start | bytes 196612
  148.7 0.9 copy-start.1
Sparse Core Ops, SparseCore 0:
  10.7 47.7 all-gather.2
  88.1 56.2 reduce-scatter.1

commit v4 on v3

--- a/solution.py
+++ b/solution.py
@@ -10,6 +10,20 @@
 COLS = (((1,), (1,)), ((), ()))
 SPAN = 512
 LANES = 128
+FOUR = 4
+
+
+def pack_kernel(query_ref, output_ref, hidden_ref, out_ref):
+    out_ref[0] = query_ref[...]
+    out_ref[1] = output_ref[...]
+    rows = out_ref.shape[1]
+    quarter = hidden_ref.shape[0] // FOUR
+    low = 0
+    for half in range(quarter // rows):
+        for four in range(FOUR):
+            first = four * quarter + half * rows
+            out_ref[2, :, low : low + LANES] = hidden_ref[first : first + rows]
+            low += LANES
 
 
 def fetch(vectors_ref, held_ref, sems):
@@ -17,7 +31,7 @@
     for low in range(0, held_ref.shape[-1], SPAN):
         codes = slice(low, low + SPAN)
         copy = pltpu.make_async_copy(
-            vectors_ref.at[:, :, :, codes], held_ref.at[:, :, :, codes], sems.at[low // SPAN]
+            vectors_ref.at[:, :2, :, codes], held_ref.at[:, :, :, codes], sems.at[low // SPAN]
         )
         copy.start()
         blocks.append((codes, copy))
@@ -57,7 +71,8 @@
     keys = keys_ref[...]
     ids = ids_ref[...]
     masks = [ids == rec for rec in range(records)]
-    first, last = ids[:1], ids[-1:]
+    first = jnp.min(ids, axis=0, keepdims=True)
+    last = jnp.max(ids, axis=0, keepdims=True)
     single = first == last
     width = own_ref.shape[1]
     for codes, copy in blocks:
@@ -117,7 +132,8 @@
     keys = keys_ref[...]
     turned = keys.T
     ids = ids_ref[...]
-    first, last = ids[:1], ids[-1:]
+    first = jnp.min(ids, axis=0, keepdims=True)
+    last = jnp.max(ids, axis=0, keepdims=True)
     masks = [ids == rec for rec in range(records)]
     width = own_ref.shape[1]
     parts = ready_ref.shape[0]
@@ -187,13 +203,50 @@
 def pre_grad_kernel(parts_ref, keys_ref, out_ref):
     keys_f = keys_ref[...].astype(jnp.float32)
     total = jnp.sum(parts_ref[...].astype(jnp.float32), axis=0)
-    own = (total * (1.0 - keys_f * keys_f)).astype(out_ref.dtype)
-    out_ref[...] = jnp.broadcast_to(own[None], out_ref.shape)
-
-
-def sum_kernel(parts_ref, out_ref):
-    own = jnp.sum(parts_ref[...].astype(jnp.float32), axis=0).astype(out_ref.dtype)
-    out_ref[...] = jnp.broadcast_to(own[None], out_ref.shape)
+    own = total * (1.0 - keys_f * keys_f)
+    toks = own.shape[0]
+    cols = LANES // FOUR
+    receivers = own.shape[1] // cols
+    copies = out_ref.shape[0] // receivers // toks
+    place = lax.broadcasted_iota(jnp.int32, (toks, LANES), 1) // cols
+    token = lax.broadcasted_iota(jnp.int32, (toks, LANES), 0) // (toks // FOUR)
+    row = 0
+    for low in range(0, own.shape[1], LANES):
+        tile = own[:, low : low + LANES]
+        turns = [tile] + [pltpu.roll(tile, cols * turn, 1) for turn in range(1, FOUR)]
+        for group in range(FOUR):
+            side = jnp.zeros_like(tile)
+            for spot in range(FOUR):
+                here = jnp.logical_and(place == spot, token == spot)
+                side = jnp.where(here, turns[(spot - group) % FOUR], side)
+            step = toks // FOUR
+            side = side + pltpu.roll(side, step, 0)
+            side = side + pltpu.roll(side, 2 * step, 0)
+            block = jnp.concatenate([side] * copies, axis=0).astype(out_ref.dtype)
+            out_ref[row : row + block.shape[0]] = block
+            row += block.shape[0]
+
+
+def weight_kernel(parts_ref, vectors_ref, out_ref, hidden_ref, sem):
+    copy = pltpu.make_async_copy(vectors_ref.at[:, 2], hidden_ref, sem)
+    copy.start()
+    seq, rows, width = hidden_ref.shape
+    parts = parts_ref[...].reshape(seq, -1, LANES)
+    copy.wait()
+    lanes = FOUR * LANES
+    total = jnp.zeros((LANES, lanes), jnp.float32)
+    for half in range(width // lanes):
+        total += lax.dot_general(
+            parts[:, half * rows : (half + 1) * rows].reshape(-1, LANES),
+            hidden_ref[:, :, half * lanes : (half + 1) * lanes].reshape(-1, lanes),
+            ROWS,
+            preferred_element_type=jnp.float32,
+        )
+    cols = LANES // FOUR
+    own = jnp.zeros((cols, LANES), jnp.float32)
+    for spot in range(FOUR):
+        own += total[spot * cols : (spot + 1) * cols, spot * LANES : (spot + 1) * LANES]
+    out_ref[...] = jnp.broadcast_to(own.astype(out_ref.dtype)[None], out_ref.shape)
 
 
 def final_kernel(
@@ -205,7 +258,7 @@
     shown = grads_ref[2 * rows :].astype(jnp.float32)
     loss_ref[...] = shown[:records] + shown[records : 2 * records]
     grad_bias_ref[...] = jnp.sum(shown[2 * records :], axis=0, keepdims=True)
-    out_ref[...] = weight_ref[...].astype(jnp.float32)
+    out_ref[...] = weight_ref[...].astype(jnp.float32).T
 
 
 def swap(parts, axis):
@@ -225,19 +278,26 @@
     tokens, feats = hidden_states.shape
     dims = key_weight.shape[1]
     rows = queries.shape[0]
-    own_toks, own_feats = tokens // label, feats // seq
+    own_toks = tokens // label
 
     few = pltpu.CompilerParams(vmem_limit_bytes=8 * 1024 * 1024)
     many = pltpu.CompilerParams(vmem_limit_bytes=52 * 1024 * 1024)
 
-    vectors = lax.all_gather(jnp.stack([queries, output_weight]), "seq", axis=0)
-    partial_pre = jnp.dot(hidden_states, key_weight, preferred_element_type=f32)
+    quarters = hidden_states.reshape(FOUR, label, -1, feats)
+    ordered = quarters.transpose(1, 0, 2, 3).reshape(tokens, feats)
+    ids = record_ids.reshape(FOUR, label, -1).transpose(1, 0, 2).reshape(tokens, 1)
+    vectors = pl.pallas_call(
+        pack_kernel,
+        out_shape=struct((3, rows, width), bf16),
+        compiler_params=pltpu.CompilerParams(vmem_limit_bytes=59 * 1024 * 1024),
+    )(queries, output_weight, hidden_states)
+    vectors = lax.all_gather(vectors, "seq", axis=0)
+    partial_pre = jnp.dot(ordered, key_weight, preferred_element_type=f32)
     pre_parts = swap(partial_pre.reshape(label, own_toks, dims), "label")
     keys_own = jnp.tanh(jnp.sum(pre_parts, axis=0)).astype(bf16)
     keys_copies = jnp.broadcast_to(keys_own[None], (label, own_toks, dims))
     keys_all = swap(keys_copies, "label").reshape(tokens, dims)
 
-    ids = record_ids[:, None]
     leader = (lax.axis_index("seq") == 0).astype(f32).reshape(1, 1)
     held = pl.BlockSpec(memory_space=pltpu.VMEM)
     far = pl.BlockSpec(memory_space=pltpu.HBM)
@@ -285,18 +345,22 @@
     grads = lax.psum_scatter(grads, "seq", scatter_dimension=0)
 
     key_parts = swap(key_grad.reshape(label, own_toks, dims), "label")
-    pre_copies = pl.pallas_call(
-        pre_grad_kernel, out_shape=struct((label, own_toks, dims), bf16), compiler_params=few
+    pre_parts = pl.pallas_call(
+        pre_grad_kernel, out_shape=struct((tokens * seq // FOUR, LANES), bf16), compiler_params=few
     )(key_parts, keys_own)
-    pre_grad = swap(pre_copies, "label").reshape(tokens, dims)
-    weight_part = lax.dot_general(
-        hidden_states, pre_grad, ROWS, preferred_element_type=f32
-    ).astype(bf16)
-    weight_parts = swap(weight_part.reshape(seq, own_feats, dims), "seq")
+    pre_parts = swap(pre_parts, ("seq", "label"))
     weight_copies = pl.pallas_call(
-        sum_kernel, out_shape=struct((seq, own_feats, dims), bf16), compiler_params=few
-    )(weight_parts)
-    weights = swap(weight_copies, "seq").reshape(feats, dims)
+        weight_kernel,
+        in_specs=[held, far],
+        out_specs=held,
+        out_shape=struct((seq, dims // seq, feats), bf16),
+        scratch_shapes=[
+            pltpu.VMEM((seq, rows, width), bf16),
+            pltpu.SemaphoreType.DMA(()),
+        ],
+        compiler_params=many,
+    )(pre_parts, vectors)
+    weights = swap(weight_copies, "seq").reshape(dims, feats)
     code_loss, grad_queries, grad_output, grad_bias, grad_key_weight = pl.pallas_call(
         final_kernel,
         out_shape=[

time: 158 us -> 159 us (level)
  Pallas kernels: 9.99 us -> 13 us
    pallas_call x2 -> x3, Pallas kernels: 0.08 us -> 3.33 us  [the longest x1 1.62 us: on_device(): pl.pallas_call(pack_kernel, out_shape=struct((3, rows, width), bf16), com...]
    all_to_all x5 -> x4, blocking collectives: 88.2 us -> 87.6 us  [swap(): return lax.all_to_all(parts, axis, 0, 0, tiled=True)]
  transfers between devices with their start and end apart: 4 -> 4, of which waited for: 3 -> 3; matrix products, arithmetic and copies ran while one was open for 1% -> 1% of each run, Pallas kernels for 0% -> 1%
where the time goes in v4:
time: 159 us; the launch traced here: 158 us
  blocking collectives  87.6 us (55%)
  waiting for transfers between devices  25.5 us (16%)
  starting transfers between devices  14.6 us (9%)
  between operations  14.2 us (9%)
  Pallas kernels  13 us (8%)
  local copies, waits for them, and re-layouts  2.83 us (2%)
    all_to_all x4, blocking collectives, swap(): return lax.all_to_all(parts, axis, 0, 0, tiled=True)  87.6 us
    all_to_all x2, waiting for transfers between devices, swap(): return lax.all_to_all(parts, axis, 0, 0, tiled=True)  21.7 us
    all_to_all x2, starting transfers between devices, swap(): return lax.all_to_all(parts, axis, 0, 0, tiled=True)  14.5 us
    pallas_call x1, Pallas kernels, on_device(): pl.pallas_call(lambda *refs: grads_kernel(records, *refs), in_specs=[held...  4.67 us
    pallas_call x1, Pallas kernels, on_device(): pl.pallas_call(lambda *refs: totals_kernel(records, *refs), in_specs=[hel...  4.14 us
    all_gather x1, waiting for transfers between devices, on_device(): vectors = lax.all_gather(vectors, 'seq', axis=0)  3.81 us
  transfers between devices with their start and end apart: 4, of which 3 were waited for; matrix products, arithmetic and copies ran while one was open for 1% of the time, Pallas kernels for 1%

profile of v4, /device:TPU:1, one launch (start us, length us, event | category | flops | bytes accessed | tf_op | source)
XLA Modules:
  0.0 158.0 jit_solution(2503590601905487521)
XLA Ops:
  7.2 0.0 copy-start
  7.2 0.0 copy-start.4
  7.2 0.0 all-gather.3.cloned.1.call-start
  7.2 1.6 %shard_map.110 = bf16[3,32,1024]{2,1,0:T(8,128)(2,1)} custom-call(bf16[32,1024]{1,0:T(8,128)(2,1)} %query_ref.1, bf16[32,1024]{1,0:T(8,128)(2,1)} %output_ref.1, bf16[256,128]{1,0:T(8,128)(2,1)} %hidden_ref.1), custom_call_target="tpu_custom_call" | custom-call | tf_op jit(solution)/shard_map/pallas_call | solution.py:289
  8.9 0.0 all-gather.3.cloned.1.call-update
  8.9 0.9 copy.17
  9.8 0.0 copy-done
  9.8 0.2 fusion
  10.0 27.8 %all_to_all.36 = f32[32,8,512]{2,1,0:T(8,128)S(1)} all-to-all(f32[32,8,512]{2,1,0:T(8,128)S(1)} %fusion), channel_id=1, replica_groups=mesh['seq'=16,'label'=32] {'label'}, dimensions={0} | all-to-all | bytes 1048576 | tf_op jit(solution)/shard_map/all_to_all | solution.py:265
  37.8 0.0 copy-start.2
  37.8 0.0 copy-start.3
  37.9 0.7 broadcast_in_dim.4
  38.6 7.5 %all-to-all-start.1 = ((bf16[32,8,512]{2,1,0:T(8,128)(2,1)}), bf16[32,8,512]{2,1,0:T(8,128)(2,1)S(1)}, u32[]{:S(2)}, u32[]{:S(2)}) async-start(bf16[32,8,512]{2,1,0:T(8,128)(2,1)} %broadcast_in_dim.4), calls=%async_computation.1 | async-start | bytes 524288 | tf_op jit(solution)/shard_map/all_to_all | solution.py:265
  46.1 0.0 copy-done.4
  46.1 0.1 reshape.45
  46.3 0.1 reshape.55.refs_2_
  46.4 9.4 %all-to-all-done.1 = bf16[32,8,512]{2,1,0:T(8,128)(2,1)S(1)} async-done(((bf16[32,8,512]{2,1,0:T(8,128)(2,1)}), bf16[32,8,512]{2,1,0:T(8,128)(2,1)S(1)}, u32[]{:S(2)}, u32[]{:S(2)}) %all-to-all-start.1) | async-done | bytes 262176 | tf_op jit(solution)/shard_map/all_to_all | solution.py:265
  55.8 3.8 %all-gather.3.cloned.1.call-done = bf16[48,32,1024]{2,1,0:T(8,128)(2,1)} async-done(((bf16[3,32,1024]{2,1,0:T(8,128)(2,1)}), bf16[48,32,1024]{2,1,0:T(8,128)(2,1)}) %all-gather.3.cloned.1.call-update) | async-done | bytes 3145744 | tf_op jit(solution)/shard_map/all_gather | solution.py:294
  59.6 4.1 %shard_map.111 = (f32[8,1024]{1,0:T(8,128)S(1)}, f32[16,4,1152]{2,1,0:T(4,128)}) custom-call(bf16[256,512]{1,0:T(8,128)(2,1)S(1)} %bitcast.19, bf16[16,3,32,1024]{3,2,1,0:T(8,128)(2,1)} %bitcast.27, s32[256,1]{1,0:T(8,128)S(1)} %reshape.55.refs_2_), custom_call_target="tpu_custom_call" | custom-call | tf_op jit(solution)/shard_map/pallas_call | solution.py:306
  63.7 7.0 %all-to-all-start.2 = ((f32[16,4,1152]{2,1,0:T(4,128)}), f32[16,4,1152]{2,1,0:T(4,128)S(1)}, u32[]{:S(2)}, u32[]{:S(2)}) async-start(f32[16,4,1152]{2,1,0:T(4,128)} %get-tuple-element.15), calls=%async_computation.2 | async-start | bytes 589824 | tf_op jit(solution)/shard_map/all_to_all | solution.py:265
  70.7 0.0 reduce-scatter.2.cloned.1.call-start
  70.8 12.3 %all-to-all-done.2.refs_4_ = f32[16,4,1152]{2,1,0:T(4,128)S(1)} async-done(((f32[16,4,1152]{2,1,0:T(4,128)}), f32[16,4,1152]{2,1,0:T(4,128)S(1)}, u32[]{:S(2)}, u32[]{:S(2)}) %all-to-all-start.2) | async-done | bytes 294944 | tf_op jit(solution)/shard_map/all_to_all | solution.py:265
  83.1 0.0 copy-done.2
  83.1 0.0 copy-done.3
  83.1 4.7 %shard_map.112 = (bf16[16,80,1024]{2,1,0:T(8,128)(2,1)}, bf16[256,512]{1,0:T(8,128)(2,1)S(1)}) custom-call(bf16[256,512]{1,0:T(8,128)(2,1)S(1)} %bitcast.20, bf16[16,3,32,1024]{3,2,1,0:T(8,128)(2,1)} %bitcast.28, s32[256,1]{1,0:T(8,128)S(1)} %reshape.55.refs_2_, f32[8,1024]{1,0:T(8,128)S(1)} %get-tuple-element.14.refs_3_, ...), custom_call_target="tpu_custom_call" | custom-call | tf_op jit(solution)/shard_map/pallas_call | solution.py:319
  87.8 0.0 reduce-scatter.2.cloned.1.call-update
  87.8 18.4 %all_to_all.37.parts_ref = bf16[32,8,512]{2,1,0:T(8,128)(2,1)S(1)} all-to-all(bf16[32,8,512]{2,1,0:T(8,128)(2,1)S(1)} %bitcast.24), channel_id=1, replica_groups=mesh['seq'=16,'label'=32] {'label'}, dimensions={0} | all-to-all | bytes 524288 | tf_op jit(solution)/shard_map/all_to_all | solution.py:265
  106.2 0.1 shard_map.113
  106.4 27.9 %all_to_all.38 = bf16[512,2,128]{2,1,0:T(2,128)(2,1)S(1)} all-to-all(bf16[512,2,128]{2,1,0:T(2,128)(2,1)S(1)} %bitcast.22), channel_id=1, replica_groups=mesh['seq'=16,'label'=32] {'seq','label'}, dimensions={0} | all-to-all | bytes 524288 | tf_op jit(solution)/shard_map/all_to_all | solution.py:265
  134.3 1.6 shard_map.114
  135.9 13.5 %all_to_all.39 = bf16[16,32,128]{2,1,0:T(8,128)(2,1)S(1)} all-to-all(bf16[16,32,128]{2,1,0:T(8,128)(2,1)S(1)} %shard_map.114), channel_id=1, replica_groups=mesh['seq'=16,'label'=32] {'seq'}, dimensions={0} | all-to-all | bytes 262144 | tf_op jit(solution)/shard_map/all_to_all | solution.py:265
  149.4 0.0 reduce-scatter.2.cloned.1.call-done
  149.4 0.0 copy-start.1
  149.4 0.9 copy-done.1
  150.3 0.8 shard_map.115
  (3 shorter events, 0.1 us)
Async XLA Ops:
  7.2 2.6 %copy-start = (bf16[128,512]{1,0:T(8,128)(2,1)S(1)}, bf16[128,512]{1,0:T(8,128)(2,1)}, u32[]{:S(2)}) copy-start(bf16[128,512]{1,0:T(8,128)(2,1)} %param.8) | copy-start | bytes 393220
  7.2 38.9 %copy-start.4 = (s32[256]{0:T(256)S(1)}, s32[256]{0:T(256)}, u32[]{:S(2)}) copy-start(s32[256]{0:T(256)} %param.12) | copy-start | bytes 3076
  7.2 52.4 %all-gather.3.cloned.1.call-start = ((), (), s32[]{:S(2)}) async-start(), calls=%async_computation.8 | async-start | bytes 3342336 | tf_op jit(solution)/shard_map/all_gather | solution.py:294
  37.8 45.3 %copy-start.2 = (s32[4,1024]{1,0:T(4,128)S(1)}, s32[4,1024]{1,0:T(4,128)}, u32[]{:S(2)}) copy-start(s32[4,1024]{1,0:T(4,128)} %refs_7_.1) | copy-start | bytes 49156
  37.8 45.3 %copy-start.3 = (f32[1024]{0:T(1024)S(1)}, f32[1024]{0:T(1024)}, u32[]{:S(2)}) copy-start(f32[1024]{0:T(1024)} %param.11) | copy-start | bytes 12292
  38.6 17.2 %all-to-all-start.1 = ((bf16[32,8,512]{2,1,0:T(8,128)(2,1)}), bf16[32,8,512]{2,1,0:T(8,128)(2,1)S(1)}, u32[]{:S(2)}, u32[]{:S(2)}) async-start(bf16[32,8,512]{2,1,0:T(8,128)(2,1)} %broadcast_in_dim.4), calls=%async_computation.1 | async-start | bytes 524288 | tf_op jit(solution)/shard_map/all_to_all | solution.py:265
  63.7 19.4 %all-to-all-start.2 = ((f32[16,4,1152]{2,1,0:T(4,128)}), f32[16,4,1152]{2,1,0:T(4,128)S(1)}, u32[]{:S(2)}, u32[]{:S(2)}) async-start(f32[16,4,1152]{2,1,0:T(4,128)} %get-tuple-element.15), calls=%async_computation.2 | async-start | bytes 589824 | tf_op jit(solution)/shard_map/all_to_all | solution.py:265
  70.7 78.6 %reduce-scatter.2.cloned.1.call-start = ((), (), s32[]{:S(2)}) async-start(), calls=%async_computation.7 | async-start | bytes 2785280 | tf_op jit(solution)/shard_map/reduce_scatter | solution.py:345
  149.4 0.9 copy-start.1
Sparse Core Ops, SparseCore 0:
  10.1 49.4 all-gather.2
  87.9 59.0 reduce-scatter.1

commit v5 on v3

--- a/solution.py
+++ b/solution.py
@@ -39,54 +39,58 @@
     return spread_vals
 
 
-def pick(wanted, rows):
-    return spread([wanted == rec for rec in range(len(rows))], rows)
-
-
 def totals_kernel(
-    records,
-    keys_ref,
-    vectors_ref,
-    ids_ref,
-    own_ref,
-    out_ref,
-    held_ref,
-    sems,
+    records, keys_ref, vectors_ref, ids_ref, own_ref, out_ref, held_ref, sems
 ):
     blocks = fetch(vectors_ref, held_ref, sems)
     keys = keys_ref[...]
     ids = ids_ref[...]
-    masks = [ids == rec for rec in range(records)]
     first, last = ids[:1], ids[-1:]
     single = first == last
+    between = jnp.max(last - first) > 1
+    heads, tails = ids == first, ids == last
     width = own_ref.shape[1]
+
+    def totals(top, expo, weighted):
+        denom = jnp.sum(expo, axis=0, keepdims=True)
+        numer = jnp.sum(weighted, axis=0, keepdims=True)
+        some = denom > 0.0
+        safe = jnp.where(some, denom, 1.0)
+        return jnp.where(some, top + jnp.log(safe), FAR), jnp.where(some, numer / safe, 0.0)
+
     for codes, copy in blocks:
         copy.wait()
         score_vals, value_vals, _, _ = products(keys, held_ref, codes)
-        tops = [
-            jnp.max(jnp.where(mask, score_vals, FAR), axis=0, keepdims=True) for mask in masks
-        ]
-        expo = jnp.exp(score_vals - spread(masks, tops))
+        head_top = jnp.max(jnp.where(heads, score_vals, FAR), axis=0, keepdims=True)
+        tail_top = jnp.max(jnp.where(tails, score_vals, FAR), axis=0, keepdims=True)
+        shifted = jnp.where(heads, score_vals - head_top, score_vals - tail_top)
+        expo = jnp.exp(jnp.where(jnp.logical_or(heads, tails), shifted, FAR))
         weighted = expo * value_vals
-        logs, means = [], []
-        for mask, top in zip(masks, tops):
-            denom = jnp.sum(jnp.where(mask, expo, 0.0), axis=0, keepdims=True)
-            numer = jnp.sum(jnp.where(mask, weighted, 0.0), axis=0, keepdims=True)
-            some = denom > 0.0
-            safe = jnp.where(some, denom, 1.0)
-            logs.append(jnp.where(some, top + jnp.log(safe), FAR))
-            means.append(jnp.where(some, numer / safe, 0.0))
-        own_ref[:, codes] = jnp.concatenate(logs + means, axis=0)
+        head_expo = jnp.where(heads, expo, 0.0)
+        head_weighted = jnp.where(heads, weighted, 0.0)
+        head_log, head_mean = totals(head_top, head_expo, head_weighted)
+        tail_log, tail_mean = totals(tail_top, expo - head_expo, weighted - head_weighted)
         table = jnp.concatenate(
             [
-                pick(first, logs),
-                jnp.where(single, FAR, pick(last, logs)),
-                pick(first, means),
-                jnp.where(single, 0.0, pick(last, means)),
+                head_log,
+                jnp.where(single, FAR, tail_log),
+                head_mean,
+                jnp.where(single, 0.0, tail_mean),
             ],
             axis=0,
         )
         out_ref[:, :, codes] = jnp.broadcast_to(table[None], (out_ref.shape[0], *table.shape))
+
+        @pl.when(between)
+        def _():
+            for rec in range(records):
+                mask = ids == rec
+                top = jnp.max(jnp.where(mask, score_vals, FAR), axis=0, keepdims=True)
+                inner = jnp.where(mask, jnp.exp(jnp.where(mask, score_vals - top, FAR)), 0.0)
+                log, mean = totals(top, inner, inner * value_vals)
+                own_ref[rec : rec + 1, codes] = log
+                own_ref[records + rec : records + rec + 1, codes] = mean
+
     marks = jnp.concatenate([first, last, first, last], axis=0).astype(jnp.float32)
     out_ref[:, :, width:] = jnp.broadcast_to(marks[None], (*out_ref.shape[:2], LANES))
 

time: 158 us -> 157 us (level)
  no operation moved by 1% of the time
where the time goes in v5:
time: 157 us
  blocking collectives  88.2 us (56%)
  waiting for transfers between devices  24.7 us (16%)
  starting transfers between devices  15.5 us (10%)
  between operations  14.2 us (9%)
  Pallas kernels  9.3 us (6%)
  local copies, waits for them, and re-layouts  1.8 us (1%)
  other arithmetic  1.61 us (1%)
    all_to_all x5, blocking collectives, swap(): return lax.all_to_all(parts, axis, 0, 0, tiled=True)  88.2 us
    all_to_all x2, waiting for transfers between devices, swap(): return lax.all_to_all(parts, axis, 0, 0, tiled=True)  21.8 us
    all_to_all x2, starting transfers between devices, swap(): return lax.all_to_all(parts, axis, 0, 0, tiled=True)  15.4 us
    pallas_call x1, Pallas kernels, on_device(): pl.pallas_call(lambda *refs: grads_kernel(records, *refs), in_specs=[held...  4.98 us
    pallas_call x1, Pallas kernels, on_device(): pl.pallas_call(lambda *refs: totals_kernel(records, *refs), in_specs=[hel...  3.43 us
  transfers between devices with their start and end apart: 4, of which 3 were waited for; matrix products, arithmetic and copies ran while one was open for 1% of the time, Pallas kernels for 0%

profile of v5, /device:TPU:1, one launch (start us, length us, event | category | flops | bytes accessed | tf_op | source)
XLA Modules:
  0.0 156.5 jit_solution(12546333078850229982)
XLA Ops:
  7.2 0.0 copy-start
  7.2 0.0 copy-start.5
  7.2 0.0 all-gather.3.cloned.1.call-start
  7.2 1.6 pad_maximum_fusion
  8.8 0.0 all-gather.3.cloned.1.call-update
  8.8 0.0 copy-done
  8.8 1.0 convolution_bitcast_fusion
  9.9 0.0 copy-start.2
  9.9 0.0 copy-start.3
  9.9 27.8 %all_to_all.35 = f32[32,8,512]{2,1,0:T(8,128)S(1)} all-to-all(f32[32,8,512]{2,1,0:T(8,128)S(1)} %convolution_bitcast_fusion), channel_id=1, replica_groups=mesh['seq'=16,'label'=32] {'label'}, dimensions={0} | all-to-all | bytes 1048576 | tf_op jit(solution)/shard_map/all_to_all | solution.py:216
  37.8 0.7 broadcast_in_dim.12
  38.5 7.5 %all-to-all-start.1 = ((bf16[32,8,512]{2,1,0:T(8,128)(2,1)}), bf16[32,8,512]{2,1,0:T(8,128)(2,1)S(1)}, u32[]{:S(2)}, u32[]{:S(2)}) async-start(bf16[32,8,512]{2,1,0:T(8,128)(2,1)} %broadcast_in_dim.12), calls=%async_computation.1 | async-start | bytes 524288 | tf_op jit(solution)/shard_map/all_to_all | solution.py:216
  46.0 0.0 copy-done.5
  46.0 0.1 copy.15.refs_2_
  46.2 9.5 %all-to-all-done.1 = bf16[32,8,512]{2,1,0:T(8,128)(2,1)S(1)} async-done(((bf16[32,8,512]{2,1,0:T(8,128)(2,1)}), bf16[32,8,512]{2,1,0:T(8,128)(2,1)S(1)}, u32[]{:S(2)}, u32[]{:S(2)}) %all-to-all-start.1) | async-done | bytes 262176 | tf_op jit(solution)/shard_map/all_to_all | solution.py:216
  55.7 2.9 %all-gather.3.cloned.1.call-done = bf16[32,32,1024]{2,1,0:T(8,128)(2,1)} async-done(((bf16[2,32,1024]{2,1,0:T(8,128)(2,1)}), bf16[32,32,1024]{2,1,0:T(8,128)(2,1)}) %all-gather.3.cloned.1.call-update) | async-done | bytes 2097168 | tf_op jit(solution)/shard_map/all_gather | solution.py:237
  58.5 3.4 %shard_map.110 = (f32[8,1024]{1,0:T(8,128)S(1)}, f32[16,4,1152]{2,1,0:T(4,128)}) custom-call(bf16[256,512]{1,0:T(8,128)(2,1)S(1)} %bitcast.23, bf16[16,2,32,1024]{3,2,1,0:T(8,128)(2,1)} %bitcast.29, s32[256,1]{1,0:T(8,128)S(1)} %copy.15.refs_2_), custom_call_target="tpu_custom_call" | custom-call | tf_op jit(solution)/shard_map/pallas_call | solution.py:250
  62.0 7.9 %all-to-all-start.2 = ((f32[16,4,1152]{2,1,0:T(4,128)}), f32[16,4,1152]{2,1,0:T(4,128)S(1)}, u32[]{:S(2)}, u32[]{:S(2)}) async-start(f32[16,4,1152]{2,1,0:T(4,128)} %get-tuple-element.15), calls=%async_computation.2 | async-start | bytes 589824 | tf_op jit(solution)/shard_map/all_to_all | solution.py:216
  69.9 0.0 reduce-scatter.2.cloned.1.call-start
  70.0 12.3 %all-to-all-done.2.refs_4_ = f32[16,4,1152]{2,1,0:T(4,128)S(1)} async-done(((f32[16,4,1152]{2,1,0:T(4,128)}), f32[16,4,1152]{2,1,0:T(4,128)S(1)}, u32[]{:S(2)}, u32[]{:S(2)}) %all-to-all-start.2) | async-done | bytes 294944 | tf_op jit(solution)/shard_map/all_to_all | solution.py:216
  82.3 0.0 copy-done.2
  82.3 0.0 copy-done.3
  82.3 5.0 %shard_map.111 = (bf16[16,80,1024]{2,1,0:T(8,128)(2,1)}, bf16[256,512]{1,0:T(8,128)(2,1)S(1)}) custom-call(bf16[256,512]{1,0:T(8,128)(2,1)S(1)} %bitcast.24, bf16[16,2,32,1024]{3,2,1,0:T(8,128)(2,1)} %bitcast.30, s32[256,1]{1,0:T(8,128)S(1)} %copy.15.refs_2_, f32[8,1024]{1,0:T(8,128)S(1)} %get-tuple-element.14.refs_3_, ...), custom_call_target="tpu_custom_call" | custom-call | tf_op jit(solution)/shard_map/pallas_call | solution.py:263
  87.3 0.0 copy-start.4
  87.3 0.0 reduce-scatter.2.cloned.1.call-update
  87.3 17.6 %all_to_all.36.parts_ref = bf16[32,8,512]{2,1,0:T(8,128)(2,1)S(1)} all-to-all(bf16[32,8,512]{2,1,0:T(8,128)(2,1)S(1)} %bitcast.26), channel_id=1, replica_groups=mesh['seq'=16,'label'=32] {'label'}, dimensions={0} | all-to-all | bytes 524288 | tf_op jit(solution)/shard_map/all_to_all | solution.py:216
  104.9 0.1 shard_map.112
  105.0 15.4 %all_to_all.37 = bf16[32,8,512]{2,1,0:T(8,128)(2,1)S(1)} all-to-all(bf16[32,8,512]{2,1,0:T(8,128)(2,1)S(1)} %shard_map.112), channel_id=1, replica_groups=mesh['seq'=16,'label'=32] {'label'}, dimensions={0} | all-to-all | bytes 524288 | tf_op jit(solution)/shard_map/all_to_all | solution.py:216
  120.3 0.0 copy-done.4
  120.3 0.2 fusion
  120.5 16.0 %all_to_all.38.parts_ref = bf16[16,8,512]{2,1,0:T(8,128)(2,1)S(1)} all-to-all(bf16[16,8,512]{2,1,0:T(8,128)(2,1)S(1)} %fusion), channel_id=1, replica_groups=mesh['seq'=16,'label'=32] {'seq'}, dimensions={0} | all-to-all | bytes 262144 | tf_op jit(solution)/shard_map/all_to_all | solution.py:216
  136.6 11.4 %all_to_all.39 = bf16[16,8,512]{2,1,0:T(8,128)(2,1)S(1)} all-to-all(bf16[16,8,512]{2,1,0:T(8,128)(2,1)S(1)} %shard_map.113), channel_id=1, replica_groups=mesh['seq'=16,'label'=32] {'seq'}, dimensions={0} | all-to-all | bytes 262144 | tf_op jit(solution)/shard_map/all_to_all | solution.py:216
  148.0 0.0 reduce-scatter.2.cloned.1.call-done
  148.0 0.0 copy-start.1
  148.0 0.9 copy-done.1
  148.9 0.8 shard_map.114
  (3 shorter events, 0.1 us)
Async XLA Ops:
  7.2 1.6 %copy-start = (bf16[128,512]{1,0:T(8,128)(2,1)S(1)}, bf16[128,512]{1,0:T(8,128)(2,1)}, u32[]{:S(2)}) copy-start(bf16[128,512]{1,0:T(8,128)(2,1)} %param.8) | copy-start | bytes 393220
  7.2 38.8 %copy-start.5 = (s32[256]{0:T(256)S(1)}, s32[256]{0:T(256)}, u32[]{:S(2)}) copy-start(s32[256]{0:T(256)} %param.12) | copy-start | bytes 3076
  7.2 51.3 %all-gather.3.cloned.1.call-start = ((), (), s32[]{:S(2)}) async-start(), calls=%async_computation.9 | async-start | bytes 2228224 | tf_op jit(solution)/shard_map/all_gather | solution.py:237
  9.9 72.4 %copy-start.2 = (s32[4,1024]{1,0:T(4,128)S(1)}, s32[4,1024]{1,0:T(4,128)}, u32[]{:S(2)}) copy-start(s32[4,1024]{1,0:T(4,128)} %refs_7_.1) | copy-start | bytes 49156
  9.9 72.4 %copy-start.3 = (f32[1024]{0:T(1024)S(1)}, f32[1024]{0:T(1024)}, u32[]{:S(2)}) copy-start(f32[1024]{0:T(1024)} %param.11) | copy-start | bytes 12292
  38.5 17.1 %all-to-all-start.1 = ((bf16[32,8,512]{2,1,0:T(8,128)(2,1)}), bf16[32,8,512]{2,1,0:T(8,128)(2,1)S(1)}, u32[]{:S(2)}, u32[]{:S(2)}) async-start(bf16[32,8,512]{2,1,0:T(8,128)(2,1)} %broadcast_in_dim.12), calls=%async_computation.1 | async-start | bytes 524288 | tf_op jit(solution)/shard_map/all_to_all | solution.py:216
  62.0 20.3 %all-to-all-start.2 = ((f32[16,4,1152]{2,1,0:T(4,128)}), f32[16,4,1152]{2,1,0:T(4,128)S(1)}, u32[]{:S(2)}, u32[]{:S(2)}) async-start(f32[16,4,1152]{2,1,0:T(4,128)} %get-tuple-element.15), calls=%async_computation.2 | async-start | bytes 589824 | tf_op jit(solution)/shard_map/all_to_all | solution.py:216
  69.9 78.1 %reduce-scatter.2.cloned.1.call-start = ((), (), s32[]{:S(2)}) async-start(), calls=%async_computation.8 | async-start | bytes 2785280 | tf_op jit(solution)/shard_map/reduce_scatter | solution.py:289
  87.3 33.0 %copy-start.4 = (bf16[256,128]{1,0:T(8,128)(2,1)S(1)}, bf16[256,128]{1,0:T(8,128)(2,1)}, u32[]{:S(2)}) copy-start(bf16[256,128]{1,0:T(8,128)(2,1)} %param.7) | copy-start | bytes 196612
  148.0 0.9 copy-start.1
Sparse Core Ops, SparseCore 0:
  10.7 47.7 all-gather.2
  87.4 56.2 reduce-scatter.1

commit v6 on v5

--- a/solution.py
+++ b/solution.py
@@ -103,7 +103,7 @@
 def grads_kernel(
     records,
     keys_ref,
-    vectors_ref,
+    held_ref,
     ids_ref,
     own_ref,
     totals_ref,
@@ -112,12 +112,9 @@
     labels_ref,
     grads_ref,
     key_grad_ref,
-    held_ref,
     ready_ref,
-    sems,
     out_sems,
 ):
-    blocks = fetch(vectors_ref, held_ref, sems)
     keys = keys_ref[...]
     turned = keys.T
     ids = ids_ref[...]
@@ -159,8 +156,8 @@
     deltas = [delta[rec : rec + 1] for rec in range(records)]
     key_grad = jnp.zeros(keys.shape, jnp.float32)
     sent = []
-    for codes, copy in blocks:
-        copy.wait()
+    for low in range(0, width, SPAN):
+        codes = slice(low, low + SPAN)
         score_vals, value_vals, query_blk, output_blk = products(keys, held_ref, codes)
         cut = lambda row_list: [row[:, codes] for row in row_list]
         pool_weight = spread(masks, cut(deltas)) * jnp.exp(score_vals - spread(masks, cut(logs)))
@@ -232,7 +229,8 @@
     own_toks, own_feats = tokens // label, feats // seq
 
     few = pltpu.CompilerParams(vmem_limit_bytes=8 * 1024 * 1024)
-    many = pltpu.CompilerParams(vmem_limit_bytes=52 * 1024 * 1024)
+    some = pltpu.CompilerParams(vmem_limit_bytes=50 * 1024 * 1024)
+    many = pltpu.CompilerParams(vmem_limit_bytes=50 * 1024 * 1024)
 
     vectors = lax.all_gather(jnp.stack([queries, output_weight]), "seq", axis=0)
     partial_pre = jnp.dot(hidden_states, key_weight, preferred_element_type=f32)
@@ -246,35 +244,33 @@
     held = pl.BlockSpec(memory_space=pltpu.VMEM)
     far = pl.BlockSpec(memory_space=pltpu.HBM)
     blocks = width // SPAN
-    vector_scratch = pltpu.VMEM((seq, 2, rows, width), bf16)
-    own_totals, totals = pl.pallas_call(
+    own_totals, totals, vectors = pl.pallas_call(
         lambda *refs: totals_kernel(records, *refs),
         in_specs=[held, far, held],
-        out_specs=[held, held],
+        out_specs=[held, held, held],
         out_shape=[
             struct((2 * records, width), f32),
             struct((seq, 4, width + LANES), f32),
+            struct(vectors.shape, bf16),
         ],
-        scratch_shapes=[vector_scratch, pltpu.SemaphoreType.DMA((blocks,))],
+        scratch_shapes=[pltpu.SemaphoreType.DMA((blocks,))],
         compiler_params=many,
     )(keys_all, vectors, ids)
     totals = swap(totals, "seq")
 
     grads, key_grad = pl.pallas_call(
         lambda *refs: grads_kernel(records, *refs),
-        in_specs=[held, far, *[held] * 6],
+        in_specs=[held] * 8,
         out_specs=[far, held],
         out_shape=[
             struct((seq, 2 * rows + 4 * records, width), bf16),
             struct((tokens, dims), bf16),
         ],
         scratch_shapes=[
-            vector_scratch,
             pltpu.VMEM((seq, 2 * rows + 4 * records, width), bf16),
             pltpu.SemaphoreType.DMA((blocks,)),
-            pltpu.SemaphoreType.DMA((blocks,)),
         ],
-        compiler_params=many,
+        compiler_params=some,
     )(
         keys_all,
         vectors,

time: 157 us -> 156 us (level)
  no operation moved by 1% of the time
where the time goes in v6:
time: 156 us
  blocking collectives  88.2 us (57%)
  waiting for transfers between devices  24.7 us (16%)
  starting transfers between devices  15.5 us (10%)
  between operations  14.2 us (9%)
  Pallas kernels  8.3 us (5%)
  local copies, waits for them, and re-layouts  1.8 us (1%)
  other arithmetic  1.61 us (1%)
    all_to_all x5, blocking collectives, swap(): return lax.all_to_all(parts, axis, 0, 0, tiled=True)  88.2 us
    all_to_all x2, waiting for transfers between devices, swap(): return lax.all_to_all(parts, axis, 0, 0, tiled=True)  21.8 us
    all_to_all x2, starting transfers between devices, swap(): return lax.all_to_all(parts, axis, 0, 0, tiled=True)  15.4 us
    pallas_call x1, Pallas kernels, on_device(): pl.pallas_call(lambda *refs: grads_kernel(records, *refs), in_specs=[held...  3.98 us
    pallas_call x1, Pallas kernels, on_device(): pl.pallas_call(lambda *refs: totals_kernel(records, *refs), in_specs=[hel...  3.43 us
  transfers between devices with their start and end apart: 4, of which 3 were waited for; matrix products, arithmetic and copies ran while one was open for 1% of the time, Pallas kernels for 0%

profile of v6, /device:TPU:1, one launch (start us, length us, event | category | flops | bytes accessed | tf_op | source)
XLA Modules:
  0.0 155.6 jit_solution(9460160284023916338)
XLA Ops:
  7.2 0.0 copy-start
  7.2 0.0 copy-start.5
  7.2 0.0 all-gather.3.cloned.1.call-start
  7.2 1.6 pad_maximum_fusion
  8.8 0.0 all-gather.3.cloned.1.call-update
  8.8 0.0 copy-done
  8.8 1.0 convolution_bitcast_fusion
  9.9 27.8 %all_to_all.35 = f32[32,8,512]{2,1,0:T(8,128)S(1)} all-to-all(f32[32,8,512]{2,1,0:T(8,128)S(1)} %convolution_bitcast_fusion), channel_id=1, replica_groups=mesh['seq'=16,'label'=32] {'label'}, dimensions={0} | all-to-all | bytes 1048576 | tf_op jit(solution)/shard_map/all_to_all | solution.py:213
  37.8 0.0 copy-start.2
  37.8 0.0 copy-start.3
  37.8 0.7 broadcast_in_dim.12
  38.5 7.5 %all-to-all-start.1 = ((bf16[32,8,512]{2,1,0:T(8,128)(2,1)}), bf16[32,8,512]{2,1,0:T(8,128)(2,1)S(1)}, u32[]{:S(2)}, u32[]{:S(2)}) async-start(bf16[32,8,512]{2,1,0:T(8,128)(2,1)} %broadcast_in_dim.12), calls=%async_computation.1 | async-start | bytes 524288 | tf_op jit(solution)/shard_map/all_to_all | solution.py:213
  46.0 0.0 copy-done.5
  46.0 0.1 copy.14.refs_2_
  46.2 9.5 %all-to-all-done.1 = bf16[32,8,512]{2,1,0:T(8,128)(2,1)S(1)} async-done(((bf16[32,8,512]{2,1,0:T(8,128)(2,1)}), bf16[32,8,512]{2,1,0:T(8,128)(2,1)S(1)}, u32[]{:S(2)}, u32[]{:S(2)}) %all-to-all-start.1) | async-done | bytes 262176 | tf_op jit(solution)/shard_map/all_to_all | solution.py:213
  55.7 2.9 %all-gather.3.cloned.1.call-done = bf16[32,32,1024]{2,1,0:T(8,128)(2,1)} async-done(((bf16[2,32,1024]{2,1,0:T(8,128)(2,1)}), bf16[32,32,1024]{2,1,0:T(8,128)(2,1)}) %all-gather.3.cloned.1.call-update) | async-done | bytes 2097168 | tf_op jit(solution)/shard_map/all_gather | solution.py:235
  58.5 3.4 %shard_map.110 = (f32[8,1024]{1,0:T(8,128)S(1)}, f32[16,4,1152]{2,1,0:T(4,128)}, bf16[16,2,32,1024]{3,2,1,0:T(8,128)(2,1)S(1)}) custom-call(bf16[256,512]{1,0:T(8,128)(2,1)S(1)} %bitcast.23, bf16[16,2,32,1024]{3,2,1,0:T(8,128)(2,1)} %bitcast.29, s32[256,1]{1,0:T(8,128)S(1)} %copy.14.refs_2_), custom_call_target="tpu_custom_call" | custom-call | tf_op jit(solution)/shard_map/pallas_call | solution.py:247
  62.0 7.9 %all-to-all-start.2 = ((f32[16,4,1152]{2,1,0:T(4,128)}), f32[16,4,1152]{2,1,0:T(4,128)S(1)}, u32[]{:S(2)}, u32[]{:S(2)}) async-start(f32[16,4,1152]{2,1,0:T(4,128)} %get-tuple-element.17), calls=%async_computation.2 | async-start | bytes 589824 | tf_op jit(solution)/shard_map/all_to_all | solution.py:213
  69.9 0.0 reduce-scatter.2.cloned.1.call-start
  70.0 12.3 %all-to-all-done.2.refs_4_ = f32[16,4,1152]{2,1,0:T(4,128)S(1)} async-done(((f32[16,4,1152]{2,1,0:T(4,128)}), f32[16,4,1152]{2,1,0:T(4,128)S(1)}, u32[]{:S(2)}, u32[]{:S(2)}) %all-to-all-start.2) | async-done | bytes 294944 | tf_op jit(solution)/shard_map/all_to_all | solution.py:213
  82.3 0.0 copy-done.2
  82.3 0.0 copy-done.3
  82.3 4.0 %shard_map.111 = (bf16[16,80,1024]{2,1,0:T(8,128)(2,1)}, bf16[256,512]{1,0:T(8,128)(2,1)S(1)}) custom-call(bf16[256,512]{1,0:T(8,128)(2,1)S(1)} %bitcast.24, bf16[16,2,32,1024]{3,2,1,0:T(8,128)(2,1)S(1)} %get-tuple-element.15.refs_1_, s32[256,1]{1,0:T(8,128)S(1)} %copy.14.refs_2_, f32[8,1024]{1,0:T(8,128)S(1)} %get-tuple-element.16.refs_3_, ...), custom_call_target="tpu_custom_call" | custom-call | tf_op jit(solution)/shard_map/pallas_call | solution.py:261
  86.3 0.0 copy-start.4
  86.3 0.0 reduce-scatter.2.cloned.1.call-update
  86.3 17.6 %all_to_all.36.parts_ref = bf16[32,8,512]{2,1,0:T(8,128)(2,1)S(1)} all-to-all(bf16[32,8,512]{2,1,0:T(8,128)(2,1)S(1)} %bitcast.26), channel_id=1, replica_groups=mesh['seq'=16,'label'=32] {'label'}, dimensions={0} | all-to-all | bytes 524288 | tf_op jit(solution)/shard_map/all_to_all | solution.py:213
  103.9 0.1 shard_map.112
  103.9 15.4 %all_to_all.37 = bf16[32,8,512]{2,1,0:T(8,128)(2,1)S(1)} all-to-all(bf16[32,8,512]{2,1,0:T(8,128)(2,1)S(1)} %shard_map.112), channel_id=1, replica_groups=mesh['seq'=16,'label'=32] {'label'}, dimensions={0} | all-to-all | bytes 524288 | tf_op jit(solution)/shard_map/all_to_all | solution.py:213
  119.3 0.0 copy-done.4
  119.3 0.2 fusion
  119.5 16.0 %all_to_all.38.parts_ref = bf16[16,8,512]{2,1,0:T(8,128)(2,1)S(1)} all-to-all(bf16[16,8,512]{2,1,0:T(8,128)(2,1)S(1)} %fusion), channel_id=1, replica_groups=mesh['seq'=16,'label'=32] {'seq'}, dimensions={0} | all-to-all | bytes 262144 | tf_op jit(solution)/shard_map/all_to_all | solution.py:213
  135.6 11.4 %all_to_all.39 = bf16[16,8,512]{2,1,0:T(8,128)(2,1)S(1)} all-to-all(bf16[16,8,512]{2,1,0:T(8,128)(2,1)S(1)} %shard_map.113), channel_id=1, replica_groups=mesh['seq'=16,'label'=32] {'seq'}, dimensions={0} | all-to-all | bytes 262144 | tf_op jit(solution)/shard_map/all_to_all | solution.py:213
  147.0 0.0 reduce-scatter.2.cloned.1.call-done
  147.0 0.0 copy-start.1
  147.0 0.9 copy-done.1
  148.0 0.8 shard_map.114
  (3 shorter events, 0.1 us)
Async XLA Ops:
  7.2 1.6 %copy-start = (bf16[128,512]{1,0:T(8,128)(2,1)S(1)}, bf16[128,512]{1,0:T(8,128)(2,1)}, u32[]{:S(2)}) copy-start(bf16[128,512]{1,0:T(8,128)(2,1)} %param.8) | copy-start | bytes 393220
  7.2 38.8 %copy-start.5 = (s32[256]{0:T(256)S(1)}, s32[256]{0:T(256)}, u32[]{:S(2)}) copy-start(s32[256]{0:T(256)} %param.12) | copy-start | bytes 3076
  7.2 51.3 %all-gather.3.cloned.1.call-start = ((), (), s32[]{:S(2)}) async-start(), calls=%async_computation.9 | async-start | bytes 2228224 | tf_op jit(solution)/shard_map/all_gather | solution.py:235
  37.8 44.5 %copy-start.2 = (s32[4,1024]{1,0:T(4,128)S(1)}, s32[4,1024]{1,0:T(4,128)}, u32[]{:S(2)}) copy-start(s32[4,1024]{1,0:T(4,128)} %refs_7_.1) | copy-start | bytes 49156
  37.8 44.5 %copy-start.3 = (f32[1024]{0:T(1024)S(1)}, f32[1024]{0:T(1024)}, u32[]{:S(2)}) copy-start(f32[1024]{0:T(1024)} %param.11) | copy-start | bytes 12292
  38.5 17.1 %all-to-all-start.1 = ((bf16[32,8,512]{2,1,0:T(8,128)(2,1)}), bf16[32,8,512]{2,1,0:T(8,128)(2,1)S(1)}, u32[]{:S(2)}, u32[]{:S(2)}) async-start(bf16[32,8,512]{2,1,0:T(8,128)(2,1)} %broadcast_in_dim.12), calls=%async_computation.1 | async-start | bytes 524288 | tf_op jit(solution)/shard_map/all_to_all | solution.py:213
  62.0 20.3 %all-to-all-start.2 = ((f32[16,4,1152]{2,1,0:T(4,128)}), f32[16,4,1152]{2,1,0:T(4,128)S(1)}, u32[]{:S(2)}, u32[]{:S(2)}) async-start(f32[16,4,1152]{2,1,0:T(4,128)} %get-tuple-element.17), calls=%async_computation.2 | async-start | bytes 589824 | tf_op jit(solution)/shard_map/all_to_all | solution.py:213
  69.9 77.1 %reduce-scatter.2.cloned.1.call-start = ((), (), s32[]{:S(2)}) async-start(), calls=%async_computation.8 | async-start | bytes 2785280 | tf_op jit(solution)/shard_map/reduce_scatter | solution.py:285
  86.3 33.0 %copy-start.4 = (bf16[256,128]{1,0:T(8,128)(2,1)S(1)}, bf16[256,128]{1,0:T(8,128)(2,1)}, u32[]{:S(2)}) copy-start(bf16[256,128]{1,0:T(8,128)(2,1)} %param.7) | copy-start | bytes 196612
  147.0 0.9 copy-start.1
Sparse Core Ops, SparseCore 0:
  10.7 47.7 all-gather.2
  86.4 56.2 reduce-scatter.1

commit v7 on v6

--- a/solution.py
+++ b/solution.py
@@ -154,35 +154,51 @@
     shown = jnp.concatenate(shown, axis=0).astype(ready_ref.dtype)
     ready_ref[:, 2 * rows :, :] = jnp.broadcast_to(shown[None], (parts, *shown.shape))
     deltas = [delta[rec : rec + 1] for rec in range(records)]
-    key_grad = jnp.zeros(keys.shape, jnp.float32)
-    sent = []
-    for low in range(0, width, SPAN):
-        codes = slice(low, low + SPAN)
-        score_vals, value_vals, query_blk, output_blk = products(keys, held_ref, codes)
-        cut = lambda row_list: [row[:, codes] for row in row_list]
-        pool_weight = spread(masks, cut(deltas)) * jnp.exp(score_vals - spread(masks, cut(logs)))
-        pool_grad = pool_weight.astype(jnp.bfloat16)
-        score_grad = (pool_weight * (value_vals - spread(masks, cut(pools)))).astype(jnp.bfloat16)
-        for half, grad in enumerate((score_grad, pool_grad)):
-            sums = jnp.dot(turned, grad, preferred_element_type=jnp.float32)
-            ready_ref[:, half * rows : (half + 1) * rows, codes] = sums.astype(
-                ready_ref.dtype
-            ).reshape(parts, rows, SPAN)
-        sent.append(
-            pltpu.make_async_copy(
-                ready_ref.at[:, :, codes], grads_ref.at[:, :, codes], out_sems.at[len(sent)]
+    def apply(over):
+        key_grad = jnp.zeros(keys.shape, jnp.float32)
+        sent = []
+        for low in range(0, width, SPAN):
+            codes = slice(low, low + SPAN)
+            score_vals, value_vals, query_blk, output_blk = products(keys, held_ref, codes)
+            cut = lambda row_list: [row[:, codes] for row in row_list]
+            pool_weight = over(cut(deltas)) * jnp.exp(score_vals - over(cut(logs)))
+            pool_grad = pool_weight.astype(jnp.bfloat16)
+            score_grad = (pool_weight * (value_vals - over(cut(pools)))).astype(jnp.bfloat16)
+            for half, grad in enumerate((score_grad, pool_grad)):
+                sums = jnp.dot(turned, grad, preferred_element_type=jnp.float32)
+                ready_ref[:, half * rows : (half + 1) * rows, codes] = sums.astype(
+                    ready_ref.dtype
+                ).reshape(parts, rows, SPAN)
+            sent.append(
+                pltpu.make_async_copy(
+                    ready_ref.at[:, :, codes], grads_ref.at[:, :, codes], out_sems.at[len(sent)]
+                )
             )
-        )
-        sent[-1].start()
-        key_grad += lax.dot_general(
-            score_grad, query_blk, COLS, preferred_element_type=jnp.float32
-        )
-        key_grad += lax.dot_general(
-            pool_grad, output_blk, COLS, preferred_element_type=jnp.float32
-        )
-    key_grad_ref[...] = key_grad.astype(key_grad_ref.dtype)
-    for copy in sent:
-        copy.wait()
+            sent[-1].start()
+            key_grad += lax.dot_general(
+                score_grad, query_blk, COLS, preferred_element_type=jnp.float32
+            )
+            key_grad += lax.dot_general(
+                pool_grad, output_blk, COLS, preferred_element_type=jnp.float32
+            )
+        key_grad_ref[...] = key_grad.astype(key_grad_ref.dtype)
+        for copy in sent:
+            copy.wait()
+
+    between = jnp.max(last - first) > 1
+    heads = ids == first
+
+    def ends(row_list):
+        picked = []
+        for end in (first, last):
+            row = row_list[-1]
+            for rec in range(records - 1):
+                row = jnp.where(end == rec, row_list[rec], row)
+            picked.append(row)
+        return jnp.where(heads, *picked)
+
+    pl.when(between)(lambda: apply(lambda row_list: spread(masks, row_list)))
+    pl.when(jnp.logical_not(between))(lambda: apply(ends))
 
 
 def pre_grad_kernel(parts_ref, keys_ref, out_ref):

time: 156 us -> 156 us (level)
  no operation moved by 1% of the time
where the time goes in v7:
time: 156 us; the launch traced here: 155 us
  blocking collectives  88.3 us (57%)
  waiting for transfers between devices  24.7 us (16%)
  starting transfers between devices  15.5 us (10%)
  between operations  14.2 us (9%)
  Pallas kernels  7.95 us (5%)
  local copies, waits for them, and re-layouts  1.8 us (1%)
  other arithmetic  1.61 us (1%)
    all_to_all x5, blocking collectives, swap(): return lax.all_to_all(parts, axis, 0, 0, tiled=True)  88.3 us
    all_to_all x2, waiting for transfers between devices, swap(): return lax.all_to_all(parts, axis, 0, 0, tiled=True)  21.8 us
    all_to_all x2, starting transfers between devices, swap(): return lax.all_to_all(parts, axis, 0, 0, tiled=True)  15.4 us
    pallas_call x1, Pallas kernels, on_device(): pl.pallas_call(lambda *refs: grads_kernel(records, *refs), in_specs=[held...  3.64 us
    pallas_call x1, Pallas kernels, on_device(): pl.pallas_call(lambda *refs: totals_kernel(records, *refs), in_specs=[hel...  3.43 us
  transfers between devices with their start and end apart: 4, of which 3 were waited for; matrix products, arithmetic and copies ran while one was open for 1% of the time, Pallas kernels for 0%

profile of v7, /device:TPU:1, one launch (start us, length us, event | category | flops | bytes accessed | tf_op | source)
XLA Modules:
  0.0 155.3 jit_solution(8377918152375253037)
XLA Ops:
  7.2 0.0 copy-start
  7.2 0.0 copy-start.5
  7.2 0.0 all-gather.3.cloned.1.call-start
  7.2 1.6 pad_maximum_fusion
  8.8 0.0 all-gather.3.cloned.1.call-update
  8.8 0.0 copy-done
  8.8 1.0 convolution_bitcast_fusion
  9.9 27.8 %all_to_all.35 = f32[32,8,512]{2,1,0:T(8,128)S(1)} all-to-all(f32[32,8,512]{2,1,0:T(8,128)S(1)} %convolution_bitcast_fusion), channel_id=1, replica_groups=mesh['seq'=16,'label'=32] {'label'}, dimensions={0} | all-to-all | bytes 1048576 | tf_op jit(solution)/shard_map/all_to_all | solution.py:229
  37.8 0.0 copy-start.2
  37.8 0.0 copy-start.3
  37.8 0.7 broadcast_in_dim.12
  38.5 7.5 %all-to-all-start.1 = ((bf16[32,8,512]{2,1,0:T(8,128)(2,1)}), bf16[32,8,512]{2,1,0:T(8,128)(2,1)S(1)}, u32[]{:S(2)}, u32[]{:S(2)}) async-start(bf16[32,8,512]{2,1,0:T(8,128)(2,1)} %broadcast_in_dim.12), calls=%async_computation.1 | async-start | bytes 524288 | tf_op jit(solution)/shard_map/all_to_all | solution.py:229
  46.0 0.0 copy-done.5
  46.0 0.1 copy.14.refs_2_
  46.2 9.5 %all-to-all-done.1 = bf16[32,8,512]{2,1,0:T(8,128)(2,1)S(1)} async-done(((bf16[32,8,512]{2,1,0:T(8,128)(2,1)}), bf16[32,8,512]{2,1,0:T(8,128)(2,1)S(1)}, u32[]{:S(2)}, u32[]{:S(2)}) %all-to-all-start.1) | async-done | bytes 262176 | tf_op jit(solution)/shard_map/all_to_all | solution.py:229
  55.7 2.9 %all-gather.3.cloned.1.call-done = bf16[32,32,1024]{2,1,0:T(8,128)(2,1)} async-done(((bf16[2,32,1024]{2,1,0:T(8,128)(2,1)}), bf16[32,32,1024]{2,1,0:T(8,128)(2,1)}) %all-gather.3.cloned.1.call-update) | async-done | bytes 2097168 | tf_op jit(solution)/shard_map/all_gather | solution.py:251
  58.5 3.4 %shard_map.110 = (f32[8,1024]{1,0:T(8,128)S(1)}, f32[16,4,1152]{2,1,0:T(4,128)}, bf16[16,2,32,1024]{3,2,1,0:T(8,128)(2,1)S(1)}) custom-call(bf16[256,512]{1,0:T(8,128)(2,1)S(1)} %bitcast.23, bf16[16,2,32,1024]{3,2,1,0:T(8,128)(2,1)} %bitcast.29, s32[256,1]{1,0:T(8,128)S(1)} %copy.14.refs_2_), custom_call_target="tpu_custom_call" | custom-call | tf_op jit(solution)/shard_map/pallas_call | solution.py:263
  62.0 7.9 %all-to-all-start.2 = ((f32[16,4,1152]{2,1,0:T(4,128)}), f32[16,4,1152]{2,1,0:T(4,128)S(1)}, u32[]{:S(2)}, u32[]{:S(2)}) async-start(f32[16,4,1152]{2,1,0:T(4,128)} %get-tuple-element.17), calls=%async_computation.2 | async-start | bytes 589824 | tf_op jit(solution)/shard_map/all_to_all | solution.py:229
  69.9 0.0 reduce-scatter.2.cloned.1.call-start
  70.0 12.3 %all-to-all-done.2.refs_4_ = f32[16,4,1152]{2,1,0:T(4,128)S(1)} async-done(((f32[16,4,1152]{2,1,0:T(4,128)}), f32[16,4,1152]{2,1,0:T(4,128)S(1)}, u32[]{:S(2)}, u32[]{:S(2)}) %all-to-all-start.2) | async-done | bytes 294944 | tf_op jit(solution)/shard_map/all_to_all | solution.py:229
  82.3 0.0 copy-done.2
  82.3 0.0 copy-done.3
  82.3 3.6 %shard_map.111 = (bf16[16,80,1024]{2,1,0:T(8,128)(2,1)}, bf16[256,512]{1,0:T(8,128)(2,1)S(1)}) custom-call(bf16[256,512]{1,0:T(8,128)(2,1)S(1)} %bitcast.24, bf16[16,2,32,1024]{3,2,1,0:T(8,128)(2,1)S(1)} %get-tuple-element.15.refs_1_, s32[256,1]{1,0:T(8,128)S(1)} %copy.14.refs_2_, f32[8,1024]{1,0:T(8,128)S(1)} %get-tuple-element.16.refs_3_, ...), custom_call_target="tpu_custom_call" | custom-call | tf_op jit(solution)/shard_map/pallas_call | solution.py:277
  85.9 0.0 copy-start.4
  85.9 0.0 reduce-scatter.2.cloned.1.call-update
  86.0 17.6 %all_to_all.36.parts_ref = bf16[32,8,512]{2,1,0:T(8,128)(2,1)S(1)} all-to-all(bf16[32,8,512]{2,1,0:T(8,128)(2,1)S(1)} %bitcast.26), channel_id=1, replica_groups=mesh['seq'=16,'label'=32] {'label'}, dimensions={0} | all-to-all | bytes 524288 | tf_op jit(solution)/shard_map/all_to_all | solution.py:229
  103.5 0.1 shard_map.112
  103.6 15.4 %all_to_all.37 = bf16[32,8,512]{2,1,0:T(8,128)(2,1)S(1)} all-to-all(bf16[32,8,512]{2,1,0:T(8,128)(2,1)S(1)} %shard_map.112), channel_id=1, replica_groups=mesh['seq'=16,'label'=32] {'label'}, dimensions={0} | all-to-all | bytes 524288 | tf_op jit(solution)/shard_map/all_to_all | solution.py:229
  119.0 0.0 copy-done.4
  119.0 0.2 fusion
  119.2 16.0 %all_to_all.38.parts_ref = bf16[16,8,512]{2,1,0:T(8,128)(2,1)S(1)} all-to-all(bf16[16,8,512]{2,1,0:T(8,128)(2,1)S(1)} %fusion), channel_id=1, replica_groups=mesh['seq'=16,'label'=32] {'seq'}, dimensions={0} | all-to-all | bytes 262144 | tf_op jit(solution)/shard_map/all_to_all | solution.py:229
  135.3 11.5 %all_to_all.39 = bf16[16,8,512]{2,1,0:T(8,128)(2,1)S(1)} all-to-all(bf16[16,8,512]{2,1,0:T(8,128)(2,1)S(1)} %shard_map.113), channel_id=1, replica_groups=mesh['seq'=16,'label'=32] {'seq'}, dimensions={0} | all-to-all | bytes 262144 | tf_op jit(solution)/shard_map/all_to_all | solution.py:229
  146.7 0.0 reduce-scatter.2.cloned.1.call-done
  146.7 0.0 copy-start.1
  146.7 0.9 copy-done.1
  147.7 0.8 shard_map.114
  (3 shorter events, 0.1 us)
Async XLA Ops:
  7.2 1.6 %copy-start = (bf16[128,512]{1,0:T(8,128)(2,1)S(1)}, bf16[128,512]{1,0:T(8,128)(2,1)}, u32[]{:S(2)}) copy-start(bf16[128,512]{1,0:T(8,128)(2,1)} %param.8) | copy-start | bytes 393220
  7.2 38.8 %copy-start.5 = (s32[256]{0:T(256)S(1)}, s32[256]{0:T(256)}, u32[]{:S(2)}) copy-start(s32[256]{0:T(256)} %param.12) | copy-start | bytes 3076
  7.2 51.3 %all-gather.3.cloned.1.call-start = ((), (), s32[]{:S(2)}) async-start(), calls=%async_computation.9 | async-start | bytes 2228224 | tf_op jit(solution)/shard_map/all_gather | solution.py:251
  37.8 44.5 %copy-start.2 = (s32[4,1024]{1,0:T(4,128)S(1)}, s32[4,1024]{1,0:T(4,128)}, u32[]{:S(2)}) copy-start(s32[4,1024]{1,0:T(4,128)} %refs_7_.1) | copy-start | bytes 49156
  37.8 44.5 %copy-start.3 = (f32[1024]{0:T(1024)S(1)}, f32[1024]{0:T(1024)}, u32[]{:S(2)}) copy-start(f32[1024]{0:T(1024)} %param.11) | copy-start | bytes 12292
  38.5 17.1 %all-to-all-start.1 = ((bf16[32,8,512]{2,1,0:T(8,128)(2,1)}), bf16[32,8,512]{2,1,0:T(8,128)(2,1)S(1)}, u32[]{:S(2)}, u32[]{:S(2)}) async-start(bf16[32,8,512]{2,1,0:T(8,128)(2,1)} %broadcast_in_dim.12), calls=%async_computation.1 | async-start | bytes 524288 | tf_op jit(solution)/shard_map/all_to_all | solution.py:229
  62.0 20.3 %all-to-all-start.2 = ((f32[16,4,1152]{2,1,0:T(4,128)}), f32[16,4,1152]{2,1,0:T(4,128)S(1)}, u32[]{:S(2)}, u32[]{:S(2)}) async-start(f32[16,4,1152]{2,1,0:T(4,128)} %get-tuple-element.17), calls=%async_computation.2 | async-start | bytes 589824 | tf_op jit(solution)/shard_map/all_to_all | solution.py:229
  69.9 76.8 %reduce-scatter.2.cloned.1.call-start = ((), (), s32[]{:S(2)}) async-start(), calls=%async_computation.8 | async-start | bytes 2785280 | tf_op jit(solution)/shard_map/reduce_scatter | solution.py:301
  85.9 33.0 %copy-start.4 = (bf16[256,128]{1,0:T(8,128)(2,1)S(1)}, bf16[256,128]{1,0:T(8,128)(2,1)}, u32[]{:S(2)}) copy-start(bf16[256,128]{1,0:T(8,128)(2,1)} %param.7) | copy-start | bytes 196612
  146.7 0.9 copy-start.1
Sparse Core Ops, SparseCore 0:
  10.7 47.7 all-gather.2
  86.1 56.2 reduce-scatter.1

commit v8 on v7

--- a/solution.py
+++ b/solution.py
@@ -176,10 +176,10 @@
             )
             sent[-1].start()
             key_grad += lax.dot_general(
-                score_grad, query_blk, COLS, preferred_element_type=jnp.float32
-            )
-            key_grad += lax.dot_general(
-                pool_grad, output_blk, COLS, preferred_element_type=jnp.float32
+                jnp.concatenate([score_grad, pool_grad], axis=1),
+                jnp.concatenate([query_blk, output_blk], axis=1),
+                COLS,
+                preferred_element_type=jnp.float32,
             )
         key_grad_ref[...] = key_grad.astype(key_grad_ref.dtype)
         for copy in sent:

time: 156 us -> 156 us (level)
  no operation moved by 1% of the time
where the time goes in v8:
time: 156 us; the launch traced here: 155 us
  blocking collectives  88.3 us (57%)
  waiting for transfers between devices  24.7 us (16%)
  starting transfers between devices  15.5 us (10%)
  between operations  14.2 us (9%)
  Pallas kernels  7.69 us (5%)
  local copies, waits for them, and re-layouts  1.8 us (1%)
  other arithmetic  1.61 us (1%)
    all_to_all x5, blocking collectives, swap(): return lax.all_to_all(parts, axis, 0, 0, tiled=True)  88.3 us
    all_to_all x2, waiting for transfers between devices, swap(): return lax.all_to_all(parts, axis, 0, 0, tiled=True)  21.8 us
    all_to_all x2, starting transfers between devices, swap(): return lax.all_to_all(parts, axis, 0, 0, tiled=True)  15.4 us
    pallas_call x1, Pallas kernels, on_device(): pl.pallas_call(lambda *refs: totals_kernel(records, *refs), in_specs=[hel...  3.43 us
    pallas_call x1, Pallas kernels, on_device(): pl.pallas_call(lambda *refs: grads_kernel(records, *refs), in_specs=[held...  3.38 us
  transfers between devices with their start and end apart: 4, of which 3 were waited for; matrix products, arithmetic and copies ran while one was open for 1% of the time, Pallas kernels for 0%

profile of v8, /device:TPU:1, one launch (start us, length us, event | category | flops | bytes accessed | tf_op | source)
XLA Modules:
  0.0 155.1 jit_solution(17919695901396641745)
XLA Ops:
  7.2 0.0 copy-start
  7.2 0.0 copy-start.5
  7.2 0.0 all-gather.3.cloned.1.call-start
  7.2 1.6 %pad_maximum_fusion = bf16[2,32,1024]{2,1,0:T(8,128)(2,1)} fusion(bf16[1,32,1024]{2,1,0:T(8,128)(2,1)} %bitcast.30, bf16[1,32,1024]{2,1,0:T(8,128)(2,1)} %bitcast.31), kind=kLoop, calls=%fused_computation.4 | loop fusion | flops 65536 | bytes 262144 | tf_op jit(solution)/shard_map/stack | solution.py:251
  8.8 0.0 all-gather.3.cloned.1.call-update
  8.8 0.0 copy-done
  8.8 1.0 convolution_bitcast_fusion
  9.9 27.8 %all_to_all.35 = f32[32,8,512]{2,1,0:T(8,128)S(1)} all-to-all(f32[32,8,512]{2,1,0:T(8,128)S(1)} %convolution_bitcast_fusion), channel_id=1, replica_groups=mesh['seq'=16,'label'=32] {'label'}, dimensions={0} | all-to-all | bytes 1048576 | tf_op jit(solution)/shard_map/all_to_all | solution.py:229
  37.8 0.0 copy-start.2
  37.8 0.0 copy-start.3
  37.8 0.7 broadcast_in_dim.12
  38.5 7.5 %all-to-all-start.1 = ((bf16[32,8,512]{2,1,0:T(8,128)(2,1)}), bf16[32,8,512]{2,1,0:T(8,128)(2,1)S(1)}, u32[]{:S(2)}, u32[]{:S(2)}) async-start(bf16[32,8,512]{2,1,0:T(8,128)(2,1)} %broadcast_in_dim.12), calls=%async_computation.1 | async-start | bytes 524288 | tf_op jit(solution)/shard_map/all_to_all | solution.py:229
  46.0 0.0 copy-done.5
  46.0 0.1 copy.14.refs_2_
  46.2 9.5 %all-to-all-done.1 = bf16[32,8,512]{2,1,0:T(8,128)(2,1)S(1)} async-done(((bf16[32,8,512]{2,1,0:T(8,128)(2,1)}), bf16[32,8,512]{2,1,0:T(8,128)(2,1)S(1)}, u32[]{:S(2)}, u32[]{:S(2)}) %all-to-all-start.1) | async-done | bytes 262176 | tf_op jit(solution)/shard_map/all_to_all | solution.py:229
  55.7 2.9 %all-gather.3.cloned.1.call-done = bf16[32,32,1024]{2,1,0:T(8,128)(2,1)} async-done(((bf16[2,32,1024]{2,1,0:T(8,128)(2,1)}), bf16[32,32,1024]{2,1,0:T(8,128)(2,1)}) %all-gather.3.cloned.1.call-update) | async-done | bytes 2097168 | tf_op jit(solution)/shard_map/all_gather | solution.py:251
  58.5 3.4 %shard_map.110 = (f32[8,1024]{1,0:T(8,128)S(1)}, f32[16,4,1152]{2,1,0:T(4,128)}, bf16[16,2,32,1024]{3,2,1,0:T(8,128)(2,1)S(1)}) custom-call(bf16[256,512]{1,0:T(8,128)(2,1)S(1)} %bitcast.23, bf16[16,2,32,1024]{3,2,1,0:T(8,128)(2,1)} %bitcast.29, s32[256,1]{1,0:T(8,128)S(1)} %copy.14.refs_2_), custom_call_target="tpu_custom_call" | custom-call | tf_op jit(solution)/shard_map/pallas_call | solution.py:263
  62.0 7.9 %all-to-all-start.2 = ((f32[16,4,1152]{2,1,0:T(4,128)}), f32[16,4,1152]{2,1,0:T(4,128)S(1)}, u32[]{:S(2)}, u32[]{:S(2)}) async-start(f32[16,4,1152]{2,1,0:T(4,128)} %get-tuple-element.17), calls=%async_computation.2 | async-start | bytes 589824 | tf_op jit(solution)/shard_map/all_to_all | solution.py:229
  69.9 0.0 reduce-scatter.2.cloned.1.call-start
  70.0 12.3 %all-to-all-done.2.refs_4_ = f32[16,4,1152]{2,1,0:T(4,128)S(1)} async-done(((f32[16,4,1152]{2,1,0:T(4,128)}), f32[16,4,1152]{2,1,0:T(4,128)S(1)}, u32[]{:S(2)}, u32[]{:S(2)}) %all-to-all-start.2) | async-done | bytes 294944 | tf_op jit(solution)/shard_map/all_to_all | solution.py:229
  82.3 0.0 copy-done.2
  82.3 0.0 copy-done.3
  82.3 3.4 %shard_map.111 = (bf16[16,80,1024]{2,1,0:T(8,128)(2,1)}, bf16[256,512]{1,0:T(8,128)(2,1)S(1)}) custom-call(bf16[256,512]{1,0:T(8,128)(2,1)S(1)} %bitcast.24, bf16[16,2,32,1024]{3,2,1,0:T(8,128)(2,1)S(1)} %get-tuple-element.15.refs_1_, s32[256,1]{1,0:T(8,128)S(1)} %copy.14.refs_2_, f32[8,1024]{1,0:T(8,128)S(1)} %get-tuple-element.16.refs_3_, ...), custom_call_target="tpu_custom_call" | custom-call | tf_op jit(solution)/shard_map/pallas_call | solution.py:277
  85.7 0.0 copy-start.4
  85.7 0.0 reduce-scatter.2.cloned.1.call-update
  85.7 17.6 %all_to_all.36.parts_ref = bf16[32,8,512]{2,1,0:T(8,128)(2,1)S(1)} all-to-all(bf16[32,8,512]{2,1,0:T(8,128)(2,1)S(1)} %bitcast.26), channel_id=1, replica_groups=mesh['seq'=16,'label'=32] {'label'}, dimensions={0} | all-to-all | bytes 524288 | tf_op jit(solution)/shard_map/all_to_all | solution.py:229
  103.3 0.1 shard_map.112
  103.3 15.4 %all_to_all.37 = bf16[32,8,512]{2,1,0:T(8,128)(2,1)S(1)} all-to-all(bf16[32,8,512]{2,1,0:T(8,128)(2,1)S(1)} %shard_map.112), channel_id=1, replica_groups=mesh['seq'=16,'label'=32] {'label'}, dimensions={0} | all-to-all | bytes 524288 | tf_op jit(solution)/shard_map/all_to_all | solution.py:229
  118.7 0.0 copy-done.4
  118.7 0.2 fusion
  118.9 16.0 %all_to_all.38.parts_ref = bf16[16,8,512]{2,1,0:T(8,128)(2,1)S(1)} all-to-all(bf16[16,8,512]{2,1,0:T(8,128)(2,1)S(1)} %fusion), channel_id=1, replica_groups=mesh['seq'=16,'label'=32] {'seq'}, dimensions={0} | all-to-all | bytes 262144 | tf_op jit(solution)/shard_map/all_to_all | solution.py:229
  135.0 11.5 %all_to_all.39 = bf16[16,8,512]{2,1,0:T(8,128)(2,1)S(1)} all-to-all(bf16[16,8,512]{2,1,0:T(8,128)(2,1)S(1)} %shard_map.113), channel_id=1, replica_groups=mesh['seq'=16,'label'=32] {'seq'}, dimensions={0} | all-to-all | bytes 262144 | tf_op jit(solution)/shard_map/all_to_all | solution.py:229
  146.5 0.0 reduce-scatter.2.cloned.1.call-done
  146.5 0.0 copy-start.1
  146.5 0.9 copy-done.1
  147.5 0.8 shard_map.114
  (3 shorter events, 0.1 us)
Async XLA Ops:
  7.2 1.6 %copy-start = (bf16[128,512]{1,0:T(8,128)(2,1)S(1)}, bf16[128,512]{1,0:T(8,128)(2,1)}, u32[]{:S(2)}) copy-start(bf16[128,512]{1,0:T(8,128)(2,1)} %param.8) | copy-start | bytes 393220
  7.2 38.8 %copy-start.5 = (s32[256]{0:T(256)S(1)}, s32[256]{0:T(256)}, u32[]{:S(2)}) copy-start(s32[256]{0:T(256)} %param.12) | copy-start | bytes 3076
  7.2 51.3 %all-gather.3.cloned.1.call-start = ((), (), s32[]{:S(2)}) async-start(), calls=%async_computation.9 | async-start | bytes 2228224 | tf_op jit(solution)/shard_map/all_gather | solution.py:251
  37.8 44.5 %copy-start.2 = (s32[4,1024]{1,0:T(4,128)S(1)}, s32[4,1024]{1,0:T(4,128)}, u32[]{:S(2)}) copy-start(s32[4,1024]{1,0:T(4,128)} %refs_7_.1) | copy-start | bytes 49156
  37.8 44.5 %copy-start.3 = (f32[1024]{0:T(1024)S(1)}, f32[1024]{0:T(1024)}, u32[]{:S(2)}) copy-start(f32[1024]{0:T(1024)} %param.11) | copy-start | bytes 12292
  38.5 17.1 %all-to-all-start.1 = ((bf16[32,8,512]{2,1,0:T(8,128)(2,1)}), bf16[32,8,512]{2,1,0:T(8,128)(2,1)S(1)}, u32[]{:S(2)}, u32[]{:S(2)}) async-start(bf16[32,8,512]{2,1,0:T(8,128)(2,1)} %broadcast_in_dim.12), calls=%async_computation.1 | async-start | bytes 524288 | tf_op jit(solution)/shard_map/all_to_all | solution.py:229
  62.0 20.3 %all-to-all-start.2 = ((f32[16,4,1152]{2,1,0:T(4,128)}), f32[16,4,1152]{2,1,0:T(4,128)S(1)}, u32[]{:S(2)}, u32[]{:S(2)}) async-start(f32[16,4,1152]{2,1,0:T(4,128)} %get-tuple-element.17), calls=%async_computation.2 | async-start | bytes 589824 | tf_op jit(solution)/shard_map/all_to_all | solution.py:229
  69.9 76.6 %reduce-scatter.2.cloned.1.call-start = ((), (), s32[]{:S(2)}) async-start(), calls=%async_computation.8 | async-start | bytes 2785280 | tf_op jit(solution)/shard_map/reduce_scatter | solution.py:301
  85.7 33.0 %copy-start.4 = (bf16[256,128]{1,0:T(8,128)(2,1)S(1)}, bf16[256,128]{1,0:T(8,128)(2,1)}, u32[]{:S(2)}) copy-start(bf16[256,128]{1,0:T(8,128)(2,1)} %param.7) | copy-start | bytes 196612
  146.5 0.9 copy-start.1
Sparse Core Ops, SparseCore 0:
  10.7 47.7 all-gather.2
  85.8 56.2 reduce-scatter.1

commit v9 on v8

--- a/solution.py
+++ b/solution.py
@@ -164,11 +164,14 @@
             pool_weight = over(cut(deltas)) * jnp.exp(score_vals - over(cut(logs)))
             pool_grad = pool_weight.astype(jnp.bfloat16)
             score_grad = (pool_weight * (value_vals - over(cut(pools)))).astype(jnp.bfloat16)
-            for half, grad in enumerate((score_grad, pool_grad)):
-                sums = jnp.dot(turned, grad, preferred_element_type=jnp.float32)
-                ready_ref[:, half * rows : (half + 1) * rows, codes] = sums.astype(
-                    ready_ref.dtype
-                ).reshape(parts, rows, SPAN)
+            both = jnp.concatenate([score_grad, pool_grad], axis=1)
+            sums = jnp.dot(turned, both, preferred_element_type=jnp.float32)
+            for half in range(2):
+                ready_ref[:, half * rows : (half + 1) * rows, codes] = (
+                    sums[:, half * SPAN : (half + 1) * SPAN]
+                    .astype(ready_ref.dtype)
+                    .reshape(parts, rows, SPAN)
+                )
             sent.append(
                 pltpu.make_async_copy(
                     ready_ref.at[:, :, codes], grads_ref.at[:, :, codes], out_sems.at[len(sent)]
@@ -176,7 +179,7 @@
             )
             sent[-1].start()
             key_grad += lax.dot_general(
-                jnp.concatenate([score_grad, pool_grad], axis=1),
+                both,
                 jnp.concatenate([query_blk, output_blk], axis=1),
                 COLS,
                 preferred_element_type=jnp.float32,

time: 156 us -> 156 us (level)
  no operation moved by 1% of the time
where the time goes in v9:
time: 156 us; the launch traced here: 155 us
  blocking collectives  88.3 us (57%)
  waiting for transfers between devices  24.7 us (16%)
  starting transfers between devices  15.5 us (10%)
  between operations  14.2 us (9%)
  Pallas kernels  7.69 us (5%)
  local copies, waits for them, and re-layouts  1.8 us (1%)
  other arithmetic  1.61 us (1%)
    all_to_all x5, blocking collectives, swap(): return lax.all_to_all(parts, axis, 0, 0, tiled=True)  88.3 us
    all_to_all x2, waiting for transfers between devices, swap(): return lax.all_to_all(parts, axis, 0, 0, tiled=True)  21.8 us
    all_to_all x2, starting transfers between devices, swap(): return lax.all_to_all(parts, axis, 0, 0, tiled=True)  15.4 us
    pallas_call x1, Pallas kernels, on_device(): pl.pallas_call(lambda *refs: totals_kernel(records, *refs), in_specs=[hel...  3.43 us
    pallas_call x1, Pallas kernels, on_device(): pl.pallas_call(lambda *refs: grads_kernel(records, *refs), in_specs=[held...  3.38 us
  transfers between devices with their start and end apart: 4, of which 3 were waited for; matrix products, arithmetic and copies ran while one was open for 1% of the time, Pallas kernels for 0%

profile of v9, /device:TPU:1, one launch (start us, length us, event | category | flops | bytes accessed | tf_op | source)
XLA Modules:
  0.0 155.1 jit_solution(17919695901396641745)
XLA Ops:
  7.2 0.0 copy-start
  7.2 0.0 copy-start.5
  7.2 0.0 all-gather.3.cloned.1.call-start
  7.2 1.6 %pad_maximum_fusion = bf16[2,32,1024]{2,1,0:T(8,128)(2,1)} fusion(bf16[1,32,1024]{2,1,0:T(8,128)(2,1)} %bitcast.30, bf16[1,32,1024]{2,1,0:T(8,128)(2,1)} %bitcast.31), kind=kLoop, calls=%fused_computation.4 | loop fusion | flops 65536 | bytes 262144 | tf_op jit(solution)/shard_map/stack | solution.py:254
  8.8 0.0 all-gather.3.cloned.1.call-update
  8.8 0.0 copy-done
  8.8 1.0 convolution_bitcast_fusion
  9.9 27.8 %all_to_all.35 = f32[32,8,512]{2,1,0:T(8,128)S(1)} all-to-all(f32[32,8,512]{2,1,0:T(8,128)S(1)} %convolution_bitcast_fusion), channel_id=1, replica_groups=mesh['seq'=16,'label'=32] {'label'}, dimensions={0} | all-to-all | bytes 1048576 | tf_op jit(solution)/shard_map/all_to_all | solution.py:232
  37.8 0.0 copy-start.2
  37.8 0.0 copy-start.3
  37.8 0.7 broadcast_in_dim.12
  38.5 7.5 %all-to-all-start.1 = ((bf16[32,8,512]{2,1,0:T(8,128)(2,1)}), bf16[32,8,512]{2,1,0:T(8,128)(2,1)S(1)}, u32[]{:S(2)}, u32[]{:S(2)}) async-start(bf16[32,8,512]{2,1,0:T(8,128)(2,1)} %broadcast_in_dim.12), calls=%async_computation.1 | async-start | bytes 524288 | tf_op jit(solution)/shard_map/all_to_all | solution.py:232
  46.0 0.0 copy-done.5
  46.0 0.1 copy.14.refs_2_
  46.2 9.5 %all-to-all-done.1 = bf16[32,8,512]{2,1,0:T(8,128)(2,1)S(1)} async-done(((bf16[32,8,512]{2,1,0:T(8,128)(2,1)}), bf16[32,8,512]{2,1,0:T(8,128)(2,1)S(1)}, u32[]{:S(2)}, u32[]{:S(2)}) %all-to-all-start.1) | async-done | bytes 262176 | tf_op jit(solution)/shard_map/all_to_all | solution.py:232
  55.7 2.9 %all-gather.3.cloned.1.call-done = bf16[32,32,1024]{2,1,0:T(8,128)(2,1)} async-done(((bf16[2,32,1024]{2,1,0:T(8,128)(2,1)}), bf16[32,32,1024]{2,1,0:T(8,128)(2,1)}) %all-gather.3.cloned.1.call-update) | async-done | bytes 2097168 | tf_op jit(solution)/shard_map/all_gather | solution.py:254
  58.5 3.4 %shard_map.110 = (f32[8,1024]{1,0:T(8,128)S(1)}, f32[16,4,1152]{2,1,0:T(4,128)}, bf16[16,2,32,1024]{3,2,1,0:T(8,128)(2,1)S(1)}) custom-call(bf16[256,512]{1,0:T(8,128)(2,1)S(1)} %bitcast.23, bf16[16,2,32,1024]{3,2,1,0:T(8,128)(2,1)} %bitcast.29, s32[256,1]{1,0:T(8,128)S(1)} %copy.14.refs_2_), custom_call_target="tpu_custom_call" | custom-call | tf_op jit(solution)/shard_map/pallas_call | solution.py:266
  62.0 7.9 %all-to-all-start.2 = ((f32[16,4,1152]{2,1,0:T(4,128)}), f32[16,4,1152]{2,1,0:T(4,128)S(1)}, u32[]{:S(2)}, u32[]{:S(2)}) async-start(f32[16,4,1152]{2,1,0:T(4,128)} %get-tuple-element.17), calls=%async_computation.2 | async-start | bytes 589824 | tf_op jit(solution)/shard_map/all_to_all | solution.py:232
  69.9 0.0 reduce-scatter.2.cloned.1.call-start
  70.0 12.3 %all-to-all-done.2.refs_4_ = f32[16,4,1152]{2,1,0:T(4,128)S(1)} async-done(((f32[16,4,1152]{2,1,0:T(4,128)}), f32[16,4,1152]{2,1,0:T(4,128)S(1)}, u32[]{:S(2)}, u32[]{:S(2)}) %all-to-all-start.2) | async-done | bytes 294944 | tf_op jit(solution)/shard_map/all_to_all | solution.py:232
  82.3 0.0 copy-done.2
  82.3 0.0 copy-done.3
  82.3 3.4 %shard_map.111 = (bf16[16,80,1024]{2,1,0:T(8,128)(2,1)}, bf16[256,512]{1,0:T(8,128)(2,1)S(1)}) custom-call(bf16[256,512]{1,0:T(8,128)(2,1)S(1)} %bitcast.24, bf16[16,2,32,1024]{3,2,1,0:T(8,128)(2,1)S(1)} %get-tuple-element.15.refs_1_, s32[256,1]{1,0:T(8,128)S(1)} %copy.14.refs_2_, f32[8,1024]{1,0:T(8,128)S(1)} %get-tuple-element.16.refs_3_, ...), custom_call_target="tpu_custom_call" | custom-call | tf_op jit(solution)/shard_map/pallas_call | solution.py:280
  85.7 0.0 copy-start.4
  85.7 0.0 reduce-scatter.2.cloned.1.call-update
  85.7 17.6 %all_to_all.36.parts_ref = bf16[32,8,512]{2,1,0:T(8,128)(2,1)S(1)} all-to-all(bf16[32,8,512]{2,1,0:T(8,128)(2,1)S(1)} %bitcast.26), channel_id=1, replica_groups=mesh['seq'=16,'label'=32] {'label'}, dimensions={0} | all-to-all | bytes 524288 | tf_op jit(solution)/shard_map/all_to_all | solution.py:232
  103.3 0.1 shard_map.112
  103.3 15.4 %all_to_all.37 = bf16[32,8,512]{2,1,0:T(8,128)(2,1)S(1)} all-to-all(bf16[32,8,512]{2,1,0:T(8,128)(2,1)S(1)} %shard_map.112), channel_id=1, replica_groups=mesh['seq'=16,'label'=32] {'label'}, dimensions={0} | all-to-all | bytes 524288 | tf_op jit(solution)/shard_map/all_to_all | solution.py:232
  118.7 0.0 copy-done.4
  118.7 0.2 fusion
  118.9 16.0 %all_to_all.38.parts_ref = bf16[16,8,512]{2,1,0:T(8,128)(2,1)S(1)} all-to-all(bf16[16,8,512]{2,1,0:T(8,128)(2,1)S(1)} %fusion), channel_id=1, replica_groups=mesh['seq'=16,'label'=32] {'seq'}, dimensions={0} | all-to-all | bytes 262144 | tf_op jit(solution)/shard_map/all_to_all | solution.py:232
  135.0 11.5 %all_to_all.39 = bf16[16,8,512]{2,1,0:T(8,128)(2,1)S(1)} all-to-all(bf16[16,8,512]{2,1,0:T(8,128)(2,1)S(1)} %shard_map.113), channel_id=1, replica_groups=mesh['seq'=16,'label'=32] {'seq'}, dimensions={0} | all-to-all | bytes 262144 | tf_op jit(solution)/shard_map/all_to_all | solution.py:232
  146.5 0.0 reduce-scatter.2.cloned.1.call-done
  146.5 0.0 copy-start.1
  146.5 0.9 copy-done.1
  147.5 0.8 shard_map.114
  (3 shorter events, 0.1 us)
Async XLA Ops:
  7.2 1.6 %copy-start = (bf16[128,512]{1,0:T(8,128)(2,1)S(1)}, bf16[128,512]{1,0:T(8,128)(2,1)}, u32[]{:S(2)}) copy-start(bf16[128,512]{1,0:T(8,128)(2,1)} %param.8) | copy-start | bytes 393220
  7.2 38.8 %copy-start.5 = (s32[256]{0:T(256)S(1)}, s32[256]{0:T(256)}, u32[]{:S(2)}) copy-start(s32[256]{0:T(256)} %param.12) | copy-start | bytes 3076
  7.2 51.3 %all-gather.3.cloned.1.call-start = ((), (), s32[]{:S(2)}) async-start(), calls=%async_computation.9 | async-start | bytes 2228224 | tf_op jit(solution)/shard_map/all_gather | solution.py:254
  37.8 44.5 %copy-start.2 = (s32[4,1024]{1,0:T(4,128)S(1)}, s32[4,1024]{1,0:T(4,128)}, u32[]{:S(2)}) copy-start(s32[4,1024]{1,0:T(4,128)} %refs_7_.1) | copy-start | bytes 49156
  37.8 44.5 %copy-start.3 = (f32[1024]{0:T(1024)S(1)}, f32[1024]{0:T(1024)}, u32[]{:S(2)}) copy-start(f32[1024]{0:T(1024)} %param.11) | copy-start | bytes 12292
  38.5 17.1 %all-to-all-start.1 = ((bf16[32,8,512]{2,1,0:T(8,128)(2,1)}), bf16[32,8,512]{2,1,0:T(8,128)(2,1)S(1)}, u32[]{:S(2)}, u32[]{:S(2)}) async-start(bf16[32,8,512]{2,1,0:T(8,128)(2,1)} %broadcast_in_dim.12), calls=%async_computation.1 | async-start | bytes 524288 | tf_op jit(solution)/shard_map/all_to_all | solution.py:232
  62.0 20.3 %all-to-all-start.2 = ((f32[16,4,1152]{2,1,0:T(4,128)}), f32[16,4,1152]{2,1,0:T(4,128)S(1)}, u32[]{:S(2)}, u32[]{:S(2)}) async-start(f32[16,4,1152]{2,1,0:T(4,128)} %get-tuple-element.17), calls=%async_computation.2 | async-start | bytes 589824 | tf_op jit(solution)/shard_map/all_to_all | solution.py:232
  69.9 76.6 %reduce-scatter.2.cloned.1.call-start = ((), (), s32[]{:S(2)}) async-start(), calls=%async_computation.8 | async-start | bytes 2785280 | tf_op jit(solution)/shard_map/reduce_scatter | solution.py:304
  85.7 33.0 %copy-start.4 = (bf16[256,128]{1,0:T(8,128)(2,1)S(1)}, bf16[256,128]{1,0:T(8,128)(2,1)}, u32[]{:S(2)}) copy-start(bf16[256,128]{1,0:T(8,128)(2,1)} %param.7) | copy-start | bytes 196612
  146.5 0.9 copy-start.1
Sparse Core Ops, SparseCore 0:
  10.7 47.7 all-gather.2
  85.8 56.2 reduce-scatter.1
